TPU v7x, 256 devices: a whole 4x4x8 slice. The times are simulated.
256 devices in a mesh: region: 64 (over y, z, core), pair: 4 (over x).
Axes of the slice: x: 4, y: 4, z: 8, core: 2. Of those that a mesh axis runs over, the one named last changes fastest.
Arguments:
- log_depth: float32 [4096, 768], P('region'), may hold values from -4 to 4
- cameras: float32 [4096, 8], P('region'), may hold values from -1 to 5.7, as said below
- pair_pose: float32 [48640, 8], P(('region', 'pair')), may hold values from -0.6 to 1.2, as said below
- depth_mean: float32 [4096, 768], P('region'), may hold values from -6 to 6
- depth_square: float32 [4096, 768], P('region'), may hold values from 1 to 30
- camera_mean: float32 [4096, 8], P('region'), may hold values from -192 to 192
- camera_square: float32 [4096, 8], P('region'), may hold values from 1000 to 30000
- pose_mean: float32 [48640, 8], P(('region', 'pair')), may hold values from -64 to 64
- pose_square: float32 [48640, 8], P(('region', 'pair')), may hold values from 100 to 3000
- pointmaps: bfloat16 [48640, 6, 768], P(('region', 'pair')), may hold values from -4 to 4
- confidence: bfloat16 [48640, 2, 768], P(('region', 'pair')), may hold values from 0.049804688 to 0.5
- pair_images: int32 [48640, 2], P(('region', 'pair')), may hold values from 0 to 4095, as said below
- pair_flag: int32 [48640], P(('region', 'pair')), may hold values from 0 to 1, as said below
Outputs:
- depth_next: float32 [4096, 768], P('region')
- camera_next: float32 [4096, 8], P('region')
- pose_next: float32 [48640, 8], P(('region', 'pair'))
- depth_mean_next: float32 [4096, 768], P(('region', 'pair'))
- depth_square_next: float32 [4096, 768], P(('region', 'pair'))
- camera_mean_next: float32 [4096, 8], P(('region', 'pair'))
- camera_square_next: float32 [4096, 8], P(('region', 'pair'))
- pose_mean_next: float32 [48640, 8], P(('region', 'pair'))
- pose_square_next: float32 [48640, 8], P(('region', 'pair'))
Inputs may be any that keep to these rules, and one draw needn't show every extreme that they name: `pair_images`: rows are held 190 to a device, devices in order region-major. The first image of a row lies in the region of the device that holds it. A temporal row's second image is (first + k) mod 4096 with 1 <= k <= 4; a loop-closure row's second image lies in another region. On every device exactly 2 loop-closure rows name a second image in each region other than its own. `pair_flag`: marks which rows of pair_images are loop closures. `cameras`: columns 0 to 3 hold a quaternion whose first entry is 0.8 to 1.2 and whose others are -0.3 to 0.3, columns 4 to 6 a translation, column 7 a log focal length of 5.3 to 5.7. `pair_pose`: columns 0 to 3 hold a quaternion whose first entry is 0.8 to 1.2 and whose others are -0.3 to 0.3, columns 4 to 6 a translation, column 7 a log scale of -0.3 to 0.3.
All inputs are finite; a program needn't handle non-finite values.
Results may differ from a plain program's by a relative error of at most 0.0003.
Values sent between devices are 32-bit elements; how exact they have to be, the bound alone decides.
A program may use at most 128 MiB of HBM per device.

v0:
```python
import jax
import jax.numpy as jnp
from jax import lax
from jax.sharding import PartitionSpec as P

ANCH_W = 32
ANCH_H = 24
ANCH = 768
CAP = 2
NEIGHBOURS = 4
ITERS = 2
START = 300


LEARN_RATE = 0.01
BETA_ONE = 0.9
BETA_TWO = 0.999
EPSILON = 1e-08


def from_behind(x, axis, by):
    count = lax.axis_size(axis)
    return lax.ppermute(x, axis, [(i, (i + by) % count) for i in range(count)])


def rotation(quaternion):
    w = quaternion[..., 0]
    x = quaternion[..., 1]
    y = quaternion[..., 2]
    z = quaternion[..., 3]
    norm_sq = w * w + x * x + y * y + z * z
    matrix = [
        [w * w + x * x - y * y - z * z, 2.0 * (x * y - w * z), 2.0 * (x * z + w * y)],
        [2.0 * (x * y + w * z), w * w - x * x + y * y - z * z, 2.0 * (y * z - w * x)],
        [2.0 * (x * z - w * y), 2.0 * (y * z + w * x), w * w - x * x - y * y + z * z],
    ]
    return [[entry / norm_sq for entry in line] for line in matrix]


def world_points(depth_log, camera):
    anchors = jnp.arange(ANCH, dtype=jnp.int32)
    across = (8 * (anchors % ANCH_W) + 4 - 4 * ANCH_W).astype(jnp.float32)
    downward = (8 * (anchors // ANCH_W) + 4 - 4 * ANCH_H).astype(jnp.float32)
    matrix = rotation(camera[:, 0:4])
    focal = jnp.exp(camera[:, 7:8])
    depth = jnp.exp(depth_log)
    local = [depth * across[None, :] / focal, depth * downward[None, :] / focal, depth]
    lines = []
    for axis_k in range(3):
        value = matrix[axis_k][0][:, None] * local[0] + matrix[axis_k][1][:, None] * local[1]
        value = value + matrix[axis_k][2][:, None] * local[2] + camera[:, 4 + axis_k][:, None]
        lines.append(value)
    return jnp.stack(lines, 1)


def pair_loss(chi_first, chi_second, pose, pointmaps, confidence, weight):
    matrix = rotation(pose[:, 0:4])
    scale = jnp.exp(pose[:, 7])[:, None, None]
    points = pointmaps.astype(jnp.float32).reshape(pose.shape[0], 2, 3, pointmaps.shape[2])
    placed = jnp.stack([chi_first, chi_second], 1)
    squares = jnp.zeros(confidence.shape, jnp.float32)
    for axis_k in range(3):
        moved = (
            matrix[axis_k][0][:, None, None] * points[:, :, 0]
            + matrix[axis_k][1][:, None, None] * points[:, :, 1]
        )
        moved = (
            moved
            + matrix[axis_k][2][:, None, None] * points[:, :, 2]
            + pose[:, 4 + axis_k][:, None, None]
        )
        gap = placed[:, :, axis_k] - scale * moved
        squares = squares + gap * gap
    return jnp.sum(weight[:, None, None] * confidence.astype(jnp.float32) * squares)


def pair_gradients(chi_first, chi_second, pose, pointmaps, confidence, weight):
    return jax.grad(pair_loss, argnums=(0, 1, 2))(
        chi_first, chi_second, pose, pointmaps, confidence, weight
    )


def adam_step(param, gradient, mean, square, step_count):
    mean = BETA_ONE * mean + (1.0 - BETA_ONE) * gradient
    square = BETA_TWO * square + (1.0 - BETA_TWO) * gradient * gradient
    fix_one = 1.0 - BETA_ONE**step_count
    fix_two = 1.0 - BETA_TWO**step_count
    param = param - LEARN_RATE * (mean / fix_one) / (jnp.sqrt(square / fix_two) + EPSILON)
    return (param, mean, square)


def spread(row_ids, values, row_total):
    one_hot = (row_ids[None, :] == jnp.arange(row_total, dtype=jnp.int32)[:, None]).astype(
        jnp.float32
    )
    flat = values.reshape(values.shape[0], -1)
    summed = jnp.dot(
        one_hot, flat, precision=lax.Precision.HIGHEST, preferred_element_type=jnp.float32
    )
    return summed.reshape((row_total,) + values.shape[1:])


def shards(
    log_depth,
    cameras,
    pair_pose,
    depth_mean,
    depth_square,
    camera_mean,
    camera_square,
    pose_mean,
    pose_square,
    pointmaps,
    confidence,
    pair_images,
    pair_flag,
):
    regions = lax.axis_size("region")
    lanes = lax.axis_size("pair")
    region = lax.axis_index("region")
    lane = lax.axis_index("pair")
    own_count = log_depth.shape[0]
    share_rows = own_count // lanes
    row_start = lane * share_rows
    capacity = CAP
    slot_total = regions * capacity
    extended = own_count + NEIGHBOURS
    firsts = pair_images[:, 0] - region * own_count
    seconds = pair_images[:, 1]
    target = seconds // own_count
    target_local = seconds - target * own_count
    is_remote = pair_flag == 1
    temporal = jnp.logical_not(is_remote)
    at_home = jnp.logical_and(temporal, target == region)
    nearby = jnp.logical_and(temporal, jnp.logical_not(at_home))
    region_ids = jnp.arange(regions, dtype=jnp.int32)
    hit_table = jnp.logical_and(is_remote[:, None], target[:, None] == region_ids[None, :]).astype(
        jnp.int32
    )
    earlier = jnp.cumsum(hit_table, 0) - hit_table
    order_rank = jnp.sum(earlier * hit_table, 1)
    slot_index = jnp.where(is_remote, target * capacity + order_rank, slot_total)
    safe_slot = jnp.where(is_remote, slot_index, 0)
    near_index = jnp.where(at_home, target_local, jnp.where(nearby, own_count + target_local, 0))
    wanted = jnp.zeros((slot_total,), jnp.int32).at[slot_index].set(target_local, mode="drop")
    asked = lax.all_to_all(
        wanted.reshape(regions, capacity), "region", split_axis=0, concat_axis=0, tiled=True
    ).reshape(slot_total)
    weight = 1.0 + pair_flag.astype(jnp.float32)
    keep_near = 1.0 - is_remote.astype(jnp.float32)
    for step_index in range(ITERS):
        edge_depth, edge_camera = from_behind(
            (log_depth[:NEIGHBOURS], cameras[:NEIGHBOURS]), "region", -1
        )
        ext_depth = jnp.concatenate([log_depth, edge_depth], 0)
        ext_camera = jnp.concatenate([cameras, edge_camera], 0)
        chi_ext, pull = jax.vjp(world_points, ext_depth, ext_camera)
        chi_first = chi_ext[firsts]
        answers = lax.all_to_all(
            chi_ext[asked].reshape(regions, capacity, 3, ANCH),
            "region",
            split_axis=0,
            concat_axis=0,
            tiled=True,
        )
        answers = answers.reshape(slot_total, 3, ANCH)
        chi_second = jnp.where(is_remote[:, None, None], answers[safe_slot], chi_ext[near_index])
        g_first, g_second, g_pose = pair_gradients(
            chi_first, chi_second, pair_pose, pointmaps, confidence, weight
        )
        outgoing = (
            jnp.zeros((slot_total, 3, ANCH), jnp.float32).at[slot_index].set(g_second, mode="drop")
        )
        returned = lax.all_to_all(
            outgoing.reshape(regions, capacity, 3, ANCH),
            "region",
            split_axis=0,
            concat_axis=0,
            tiled=True,
        )
        row_ids = jnp.concatenate([firsts, near_index, asked])
        values = jnp.concatenate(
            [g_first, g_second * keep_near[:, None, None], returned.reshape(slot_total, 3, ANCH)], 0
        )
        g_depth, g_camera = pull(spread(row_ids, values, extended))
        back_depth, back_camera = from_behind(
            (g_depth[own_count:], g_camera[own_count:]), "region", 1
        )
        grad_depth = jnp.concatenate(
            [g_depth[:NEIGHBOURS] + back_depth, g_depth[NEIGHBOURS:own_count]], 0
        )
        grad_camera = jnp.concatenate(
            [g_camera[:NEIGHBOURS] + back_camera, g_camera[NEIGHBOURS:own_count]], 0
        )
        step_count = START + step_index + 1
        grad_depth, grad_camera = lax.psum((grad_depth, grad_camera), "pair")
        log_depth, depth_mean, depth_square = adam_step(
            log_depth, grad_depth, depth_mean, depth_square, step_count
        )
        cameras, camera_mean, camera_square = adam_step(
            cameras, grad_camera, camera_mean, camera_square, step_count
        )
        pair_pose, pose_mean, pose_square = adam_step(
            pair_pose, g_pose, pose_mean, pose_square, step_count
        )
    depth_mean = lax.dynamic_slice_in_dim(depth_mean, row_start, share_rows, 0)
    depth_square = lax.dynamic_slice_in_dim(depth_square, row_start, share_rows, 0)
    camera_mean = lax.dynamic_slice_in_dim(camera_mean, row_start, share_rows, 0)
    camera_square = lax.dynamic_slice_in_dim(camera_square, row_start, share_rows, 0)
    return (
        log_depth,
        cameras,
        pair_pose,
        depth_mean,
        depth_square,
        camera_mean,
        camera_square,
        pose_mean,
        pose_square,
    )


def solution(mesh):
    placed = (
        P("region", None),
        P("region", None),
        P(("region", "pair"), None),
        P("region", None),
        P("region", None),
        P("region", None),
        P("region", None),
        P(("region", "pair"), None),
        P(("region", "pair"), None),
        P(("region", "pair"), None, None),
        P(("region", "pair"), None, None),
        P(("region", "pair"), None),
        P(("region", "pair")),
    )
    return jax.shard_map(
        shards,
        mesh=mesh,
        in_specs=placed,
        out_specs=(
            P("region", None),
            P("region", None),
            P(("region", "pair"), None),
            P(("region", "pair"), None),
            P(("region", "pair"), None),
            P(("region", "pair"), None),
            P(("region", "pair"), None),
            P(("region", "pair"), None),
            P(("region", "pair"), None),
        ),
        check_vma=False,
    )
```

profile of v0, /device:TPU:4, one launch (start us, length us, event | category | flops | bytes accessed | tf_op | source)
XLA Modules:
  0.0 475.0 jit_solution(1413014152998293438)
XLA Ops:
  7.2 7.8 %collective-permute-start = (f32[4,8]{0,1:T(8,128)}, f32[4,8]{0,1:T(8,128)S(1)}, u32[]{:S(2)}, u32[]{:S(2)}) collective-permute-start(f32[4,8]{0,1:T(8,128)} %bitcast.949), channel_id=1, source_target_pairs={{0,252},{4,0},{8,4},{12,8},{16,12},{20,16},{24,20},{28,24},{32,28}... | collective-permute-start | bytes 392 | tf_op jit(solution)/shard_map/ppermute | solution.py:23
  30.4 6.8 %all-to-all-done = s32[64,1,2]{2,1,0:T(1,128)S(1)} async-done(((s32[64,1,2]{2,1,0:T(1,128)}), s32[64,1,2]{2,1,0:T(1,128)S(1)}, u32[]{:S(2)}, u32[]{:S(2)}) %all-to-all-start) | async-done | bytes 544 | tf_op jit(solution)/shard_map/all_to_all | solution.py:146
  42.4 5.7 %all-to-all-start.1 = ((f32[64,2,3,768]{3,1,2,0:T(2,128)}), f32[64,2,3,768]{3,1,2,0:T(2,128)}, u32[]{:S(2)}, u32[]{:S(2)}) async-start(f32[64,2,3,768]{3,1,2,0:T(2,128)} %copy.223), calls=%async_computation.1 | async-start | bytes 2359296 | tf_op jit(solution)/shard_map/all_to_all | solution.py:159
  60.4 4.7 gather_fusion
  65.0 13.8 %all-to-all-done.1 = f32[64,2,3,768]{3,1,2,0:T(2,128)} async-done(((f32[64,2,3,768]{3,1,2,0:T(2,128)}), f32[64,2,3,768]{3,1,2,0:T(2,128)}, u32[]{:S(2)}, u32[]{:S(2)}) %all-to-all-start.1) | async-done | bytes 1179680 | tf_op jit(solution)/shard_map/all_to_all | solution.py:159
  81.7 4.9 %gather_fusion.2 = f32[190,3,768]{2,1,0:T(4,128)} fusion(f32[128,3,768]{2,1,0:T(4,128)} %bitcast.913, s32[1024]{0:T(1024)} %pad_clamp_fusion.1), kind=kCustom, calls=%fused_computation.2 | custom fusion | bytes 3502840 | tf_op jit(solution)/shard_map/gather | solution.py:167
  103.6 25.8 %scatter_fusion = f32[128,3,768]{2,1,0:T(4,128)} fusion(f32[128,3,768]{2,1,0:T(4,128)} %broadcast.1460.clone, s32[190]{0:T(256)} %copy-done.63, f32[190,3,768]{2,1,0:T(4,128)} %copy.232), kind=kCustom, calls=%fused_computation.9 | custom fusion | bytes 5253880 | tf_op jit(solution)/shard_map/scatter | solution.py:172
  132.6 7.0 %all-to-all-start.2 = ((f32[64,2,3,768]{3,1,2,0:T(2,128)}), f32[64,2,3,768]{3,1,2,0:T(2,128)}, u32[]{:S(2)}, u32[]{:S(2)}) async-start(f32[64,2,3,768]{3,1,2,0:T(2,128)} %copy.234), calls=%async_computation.2 | async-start | bytes 2359296 | tf_op jit(solution)/shard_map/all_to_all | solution.py:174
  154.7 15.7 %all-to-all-done.2 = f32[64,2,3,768]{3,1,2,0:T(2,128)} async-done(((f32[64,2,3,768]{3,1,2,0:T(2,128)}), f32[64,2,3,768]{3,1,2,0:T(2,128)}, u32[]{:S(2)}, u32[]{:S(2)}) %all-to-all-start.2) | async-done | bytes 1179680 | tf_op jit(solution)/shard_map/all_to_all | solution.py:174
  176.1 6.1 %copy.236 = f32[2304,508]{1,0:T(8,128)} copy(f32[2304,508]{0,1:T(8,128)} %maximum_bitcast_fusion) | data formatting | bytes 9363456 | tf_op jit(solution)/shard_map/dot_general | solution.py:97
  182.3 5.0 %fusion.59 = f32[68,3,768]{2,0,1:T(8,128)S(1)} fusion(f32[3,768,508]{2,1,0:T(8,128)} %bitcast.909, s32[508]{0:T(512)} %pad_add_fusion.8), kind=kOutput, calls=%fused_computation.202 | convolution fusion | flops 955107072 | bytes 5310448 | tf_op jit(solution)/shard_map/dot_general | solution.py:97
  195.8 8.9 %psum.29 = f32[64,8]{0,1:T(8,128)} all-reduce(f32[64,8]{0,1:T(8,128)} %pad_maximum_fusion.11), channel_id=1, replica_groups=mesh['region'=64,'pair'=4] {'pair'}, use_global_device_ids=true, to_apply=%region_20.21 | all-reduce | flops 512 | bytes 4096 | tf_op jit(solution)/shard_map/psum | solution.py:196
  208.5 4.9 %collective-permute-done.2 = f32[4,768]{1,0:T(4,128)S(1)} collective-permute-done((f32[4,768]{1,0:T(4,128)}, f32[4,768]{1,0:T(4,128)S(1)}, u32[]{:S(2)}, u32[]{:S(2)}) %collective-permute-start.2) | collective-permute-done | bytes 12320 | tf_op jit(solution)/shard_map/ppermute | solution.py:23
  216.4 38.1 %all-reduce.46.cloned.1.call-done = f32[64,768]{1,0:T(8,128)} async-done(((f32[64,768]{1,0:T(8,128)}), f32[64,768]{1,0:T(8,128)}) %all-reduce.46.cloned.1.call-update) | async-done | bytes 196624 | tf_op jit(solution)/shard_map/psum | solution.py:196
  269.9 7.8 %all-to-all-start.3 = ((f32[64,2,3,768]{3,1,2,0:T(2,128)}), f32[64,2,3,768]{3,1,2,0:T(2,128)}, u32[]{:S(2)}, u32[]{:S(2)}) async-start(f32[64,2,3,768]{3,1,2,0:T(2,128)} %copy.239), calls=%async_computation.3 | async-start | bytes 2359296 | tf_op jit(solution)/shard_map/all_to_all | solution.py:159
  295.3 13.2 %all-to-all-done.3 = f32[64,2,3,768]{3,1,2,0:T(2,128)} async-done(((f32[64,2,3,768]{3,1,2,0:T(2,128)}), f32[64,2,3,768]{3,1,2,0:T(2,128)}, u32[]{:S(2)}, u32[]{:S(2)}) %all-to-all-start.3) | async-done | bytes 1179680 | tf_op jit(solution)/shard_map/all_to_all | solution.py:159
  311.4 4.9 %gather_fusion.6 = f32[190,3,768]{2,1,0:T(4,128)} fusion(f32[128,3,768]{2,1,0:T(4,128)} %bitcast.912, s32[1024]{0:T(1024)} %pad_clamp_fusion.1), kind=kCustom, calls=%fused_computation.6 | custom fusion | bytes 3502840 | tf_op jit(solution)/shard_map/gather | solution.py:167
  332.5 17.4 %scatter_fusion.1 = f32[128,3,768]{2,1,0:T(4,128)S(1)} fusion(f32[128,3,768]{2,1,0:T(4,128)S(1)} %broadcast.1460, s32[190]{0:T(256)S(1)} %copy-done.64, f32[190,3,768]{2,1,0:T(4,128)} %copy.244), kind=kCustom, calls=%fused_computation.10 | custom fusion | bytes 5253880 | tf_op jit(solution)/shard_map/scatter | solution.py:172
  351.6 7.0 %all-to-all-start.4 = ((f32[64,2,3,768]{3,1,2,0:T(2,128)}), f32[64,2,3,768]{3,1,2,0:T(2,128)}, u32[]{:S(2)}, u32[]{:S(2)}) async-start(f32[64,2,3,768]{3,1,2,0:T(2,128)} %copy.246), calls=%async_computation.4 | async-start | bytes 2359296 | tf_op jit(solution)/shard_map/all_to_all | solution.py:174
  366.8 22.6 %all-to-all-done.4 = f32[64,2,3,768]{3,1,2,0:T(2,128)} async-done(((f32[64,2,3,768]{3,1,2,0:T(2,128)}), f32[64,2,3,768]{3,1,2,0:T(2,128)}, u32[]{:S(2)}, u32[]{:S(2)}) %all-to-all-start.4) | async-done | bytes 1179680 | tf_op jit(solution)/shard_map/all_to_all | solution.py:174
  395.0 6.1 %copy.248 = f32[2304,508]{1,0:T(8,128)} copy(f32[2304,508]{0,1:T(8,128)} %maximum_bitcast_fusion.1) | data formatting | bytes 9363456 | tf_op jit(solution)/shard_map/dot_general | solution.py:97
  401.1 5.0 %fusion.57 = f32[68,3,768]{2,0,1:T(8,128)S(1)} fusion(f32[3,768,508]{2,1,0:T(8,128)} %bitcast.908, s32[508]{0:T(512)S(1)} %copy-done.44), kind=kOutput, calls=%fused_computation.201 | convolution fusion | flops 955107072 | bytes 5310448 | tf_op jit(solution)/shard_map/dot_general | solution.py:97
  414.1 8.0 %psum.31 = f32[64,8]{0,1:T(8,128)S(1)} all-reduce(f32[64,8]{0,1:T(8,128)S(1)} %pad_maximum_fusion.13), channel_id=1, replica_groups=mesh['region'=64,'pair'=4] {'pair'}, use_global_device_ids=true, to_apply=%region_52.53 | all-reduce | flops 512 | bytes 4096 | tf_op jit(solution)/shard_map/psum | solution.py:196
  424.8 39.9 %all-reduce.48.cloned.1.call-done = f32[64,768]{1,0:T(8,128)} async-done(((f32[64,768]{1,0:T(8,128)}), f32[64,768]{1,0:T(8,128)}) %all-reduce.48.cloned.1.call-update) | async-done | bytes 196624 | tf_op jit(solution)/shard_map/psum | solution.py:196
  (488 shorter events, 170.9 us)
Async XLA Ops:
  7.2 31.4 %copy-start.5 = (f32[64,768]{1,0:T(8,128)S(1)}, f32[64,768]{1,0:T(8,128)}, u32[]{:S(2)}) copy-start(f32[64,768]{1,0:T(8,128)} %param.13) | copy-start | bytes 589828
  7.2 20.6 %collective-permute-start = (f32[4,8]{0,1:T(8,128)}, f32[4,8]{0,1:T(8,128)S(1)}, u32[]{:S(2)}, u32[]{:S(2)}) collective-permute-start(f32[4,8]{0,1:T(8,128)} %bitcast.949), channel_id=1, source_target_pairs={{0,252},{4,0},{8,4},{12,8},{16,12},{20,16},{24,20},{28,24},{32,28}... | collective-permute-start | bytes 392 | tf_op jit(solution)/shard_map/ppermute | solution.py:23
  15.7 21.6 %collective-permute-start.1 = (f32[4,768]{1,0:T(4,128)S(1)}, f32[4,768]{1,0:T(4,128)S(1)}, u32[]{:S(2)}, u32[]{:S(2)}) collective-permute-start(f32[4,768]{1,0:T(4,128)S(1)} %slice.243), channel_id=1, source_target_pairs={{0,252},{4,0},{8,4},{12,8},{16,12},{20,16},{24,20},{28,24},{32,28}... | collective-permute-start | bytes 36872 | tf_op jit(solution)/shard_map/ppermute | solution.py:23
  17.7 20.8 %copy-start.43 = (pred[190]{0:T(512)(128)(4,1)}, pred[190]{0:T(512)(128)(4,1)S(1)}, u32[]{:S(2)}) copy-start(pred[190]{0:T(512)(128)(4,1)S(1)} %get-tuple-element.141) | copy-start | bytes 574
  23.2 14.0 %all-to-all-start = ((s32[64,1,2]{2,1,0:T(1,128)}), s32[64,1,2]{2,1,0:T(1,128)S(1)}, u32[]{:S(2)}, u32[]{:S(2)}) async-start(s32[64,1,2]{2,1,0:T(1,128)} %bitcast.5), calls=%async_computation | async-start | bytes 65536 | tf_op jit(solution)/shard_map/all_to_all | solution.py:146
  42.4 36.4 %all-to-all-start.1 = ((f32[64,2,3,768]{3,1,2,0:T(2,128)}), f32[64,2,3,768]{3,1,2,0:T(2,128)}, u32[]{:S(2)}, u32[]{:S(2)}) async-start(f32[64,2,3,768]{3,1,2,0:T(2,128)} %copy.223), calls=%async_computation.1 | async-start | bytes 2359296 | tf_op jit(solution)/shard_map/all_to_all | solution.py:159
  132.6 37.8 %all-to-all-start.2 = ((f32[64,2,3,768]{3,1,2,0:T(2,128)}), f32[64,2,3,768]{3,1,2,0:T(2,128)}, u32[]{:S(2)}, u32[]{:S(2)}) async-start(f32[64,2,3,768]{3,1,2,0:T(2,128)} %copy.234), calls=%async_computation.2 | async-start | bytes 2359296 | tf_op jit(solution)/shard_map/all_to_all | solution.py:174
  139.6 114.8 %all-reduce.46.cloned.1.call-start = ((), (), s32[]{:S(2)}) async-start(), calls=%async_computation.5 | async-start | bytes 393216 | tf_op jit(solution)/shard_map/psum | solution.py:196
  188.7 6.4 %collective-permute-start.3 = (f32[4,8]{0,1:T(8,128)S(1)}, f32[4,8]{0,1:T(8,128)S(1)}, u32[]{:S(2)}, u32[]{:S(2)}) collective-permute-start(f32[4,8]{0,1:T(8,128)S(1)} %slice.269), channel_id=1, source_target_pairs={{0,4},{4,8},{8,12},{12,16},{16,20},{20,24},{24,28},{28,32},{32,36}... | collective-permute-start | bytes 392 | tf_op jit(solution)/shard_map/ppermute | solution.py:23
  205.4 1.8 collective-permute-start.4
  206.5 6.9 %collective-permute-start.2 = (f32[4,768]{1,0:T(4,128)}, f32[4,768]{1,0:T(4,128)S(1)}, u32[]{:S(2)}, u32[]{:S(2)}) collective-permute-start(f32[4,768]{1,0:T(4,128)} %slice.323), channel_id=1, source_target_pairs={{0,4},{4,8},{8,12},{12,16},{16,20},{20,24},{24,28},{28,32},{32,36}... | collective-permute-start | bytes 36872 | tf_op jit(solution)/shard_map/ppermute | solution.py:23
  255.8 4.7 collective-permute-start.5
  269.9 38.6 %all-to-all-start.3 = ((f32[64,2,3,768]{3,1,2,0:T(2,128)}), f32[64,2,3,768]{3,1,2,0:T(2,128)}, u32[]{:S(2)}, u32[]{:S(2)}) async-start(f32[64,2,3,768]{3,1,2,0:T(2,128)} %copy.239), calls=%async_computation.3 | async-start | bytes 2359296 | tf_op jit(solution)/shard_map/all_to_all | solution.py:159
  351.6 37.8 %all-to-all-start.4 = ((f32[64,2,3,768]{3,1,2,0:T(2,128)}), f32[64,2,3,768]{3,1,2,0:T(2,128)}, u32[]{:S(2)}, u32[]{:S(2)}) async-start(f32[64,2,3,768]{3,1,2,0:T(2,128)} %copy.246), calls=%async_computation.4 | async-start | bytes 2359296 | tf_op jit(solution)/shard_map/all_to_all | solution.py:174
  358.6 106.1 %all-reduce.48.cloned.1.call-start = ((), (), s32[]{:S(2)}) async-start(), calls=%async_computation.6 | async-start | bytes 393216 | tf_op jit(solution)/shard_map/psum | solution.py:196
  407.0 15.0 %copy-start.39 = (f32[64,8]{0,1:T(8,128)S(1)}, f32[64,8]{0,1:T(8,128)}, u32[]{:S(2)}) copy-start(f32[64,8]{0,1:T(8,128)} %copy-done.38) | copy-start | bytes 6148
  407.1 15.0 %copy-start.40 = (f32[64,8]{0,1:T(8,128)S(1)}, f32[64,8]{0,1:T(8,128)}, u32[]{:S(2)}) copy-start(f32[64,8]{0,1:T(8,128)} %psum.29) | copy-start | bytes 6148
  407.1 15.0 %copy-start.48 = (f32[64,8]{0,1:T(8,128)S(1)}, f32[64,8]{0,1:T(8,128)}, u32[]{:S(2)}) copy-start(f32[64,8]{0,1:T(8,128)} %param.18) | copy-start | bytes 6148
  407.1 15.0 %copy-start.49 = (f32[64,8]{0,1:T(8,128)S(1)}, f32[64,8]{0,1:T(8,128)}, u32[]{:S(2)}) copy-start(f32[64,8]{0,1:T(8,128)} %param.19) | copy-start | bytes 6148
  407.4 57.3 %copy-start.20 = (f32[64,768]{1,0:T(8,128)S(1)}, f32[64,768]{1,0:T(8,128)}, u32[]{:S(2)}) copy-start(f32[64,768]{1,0:T(8,128)} %param.16) | copy-start | bytes 589828
  407.4 57.3 %copy-start.21 = (f32[64,768]{1,0:T(8,128)S(1)}, f32[64,768]{1,0:T(8,128)}, u32[]{:S(2)}) copy-start(f32[64,768]{1,0:T(8,128)} %param.17) | copy-start | bytes 589828
  407.4 57.3 %copy-start.22 = (f32[64,768]{1,0:T(8,128)S(1)}, f32[64,768]{1,0:T(8,128)}, u32[]{:S(2)}) copy-start(f32[64,768]{1,0:T(8,128)} %all-reduce.46.cloned.1.call-done) | copy-start | bytes 589828
  407.7 6.4 %collective-permute-start.7 = (f32[4,8]{0,1:T(8,128)S(1)}, f32[4,8]{0,1:T(8,128)S(1)}, u32[]{:S(2)}, u32[]{:S(2)}) collective-permute-start(f32[4,8]{0,1:T(8,128)S(1)} %slice.299), channel_id=1, source_target_pairs={{0,4},{4,8},{8,12},{12,16},{16,20},{20,24},{24,28},{28,32},{32,36}... | collective-permute-start | bytes 392 | tf_op jit(solution)/shard_map/ppermute | solution.py:23
  408.5 14.2 %collective-permute-start.6 = (f32[4,768]{1,0:T(4,128)S(1)}, f32[4,768]{1,0:T(4,128)S(1)}, u32[]{:S(2)}, u32[]{:S(2)}) collective-permute-start(f32[4,768]{1,0:T(4,128)S(1)} %slice.335), channel_id=1, source_target_pairs={{0,4},{4,8},{8,12},{12,16},{16,20},{20,24},{24,28},{28,32},{32,36}... | collective-permute-start | bytes 36872 | tf_op jit(solution)/shard_map/ppermute | solution.py:23
  (150 other events, 402.2 us)
Sparse Core Ops, SparseCore 0:
  215.0 39.4 all-reduce.45
  423.6 41.0 all-reduce.47
where the time goes:
time: 484 us; the launch traced here: 475 us
  waiting for transfers between devices  164 us (34%)
  local copies, waits for them, and re-layouts  150 us (31%)
  other arithmetic  69.6 us (14%)
  starting transfers between devices  47.4 us (10%)
  between operations  17 us (4%)
  blocking collectives  16.9 us (3%)
  matrix products  9.93 us (2%)
    psum x2, waiting for transfers between devices, shards(): grad_depth, grad_camera = lax.psum((grad_depth, grad_camera), 'pair')  78 us
    scatter x2, local copies, waits for them, and re-layouts, shards(): jnp.zeros((slot_total, 3, ANCH), jnp.float32).at[slot_index]  43.3 us
    all_to_all x2, waiting for transfers between devices, shards(): lax.all_to_all(outgoing.reshape(regions, capacity, 3, ANCH), 'region', sp...  38.3 us
    all_to_all x2, waiting for transfers between devices, shards(): lax.all_to_all(chi_ext[asked].reshape(regions, capacity, 3, ANCH), 'regio...  27 us
    psum x2, blocking collectives, shards(): grad_depth, grad_camera = lax.psum((grad_depth, grad_camera), 'pair')  16.9 us
    another operation x8, local copies, waits for them, and re-layouts, pair_loss(): placed = jnp.stack([chi_first, chi_second], 1)  16.3 us
    ppermute x8, starting transfers between devices, from_behind(): return lax.ppermute(x, axis, [(i, (i + by) % count) for i in range(count)])  14.6 us
    all_to_all x2, starting transfers between devices, shards(): lax.all_to_all(outgoing.reshape(regions, capacity, 3, ANCH), 'region', sp...  14 us
  transfers between devices with their start and end apart: 15, of which 10 were waited for; matrix products, arithmetic and copies ran while one was open for 15% of the time, Pallas kernels for 0%

commit v1 on v0

v1 whole, which is shorter than its diff:
```python
import functools

import jax
import jax.numpy as jnp
from jax import lax
from jax.experimental import pallas as pl
from jax.experimental.pallas import tpu as pltpu
from jax.sharding import PartitionSpec as P

ANCH_W = 32
ANCH_H = 24
ANCH = 768
CAP = 2
NEIGHBOURS = 4
ITERS = 2
START = 300

LEARN_RATE = 0.01
BETA_ONE = 0.9
BETA_TWO = 0.999
EPSILON = 1e-08

TILES = ANCH // 128
EDGE = 8
MSG = 16
F32 = jnp.float32
BF16 = jnp.bfloat16


def rounded(value, multiple):
    return -(-value // multiple) * multiple


def split_two(x):
    high = x.astype(BF16)
    return high, (x - high.astype(F32)).astype(BF16)


def split_three(x):
    high = x.astype(BF16)
    rest = x - high.astype(F32)
    middle = rest.astype(BF16)
    return high, middle, (rest - middle.astype(F32)).astype(BF16)


def dot(a, b):
    return jnp.dot(a, b, preferred_element_type=F32)


def dot_exact(one_hot, x):
    high, middle, low = split_three(x)
    return dot(one_hot, high) + (dot(one_hot, middle) + dot(one_hot, low))


def rotation_rows(w, x, y, z):
    inverse = 1.0 / (w * w + x * x + y * y + z * z)
    matrix = [
        [w * w + x * x - y * y - z * z, 2.0 * (x * y - w * z), 2.0 * (x * z + w * y)],
        [2.0 * (x * y + w * z), w * w - x * x + y * y - z * z, 2.0 * (y * z - w * x)],
        [2.0 * (x * z - w * y), 2.0 * (y * z + w * x), w * w - x * x - y * y + z * z],
    ]
    return [[entry * inverse for entry in line] for line in matrix], inverse


def rotation_pull(q, matrix, inverse, g):
    w, x, y, z = q
    along = sum(g[k][j] * matrix[k][j] for k in range(3) for j in range(3))
    diag = g[0][0] + g[1][1] + g[2][2]
    g_w = w * diag + z * (g[1][0] - g[0][1]) + y * (g[0][2] - g[2][0]) + x * (g[2][1] - g[1][2])
    g_x = (
        x * (g[0][0] - g[1][1] - g[2][2])
        + y * (g[0][1] + g[1][0])
        + z * (g[0][2] + g[2][0])
        + w * (g[2][1] - g[1][2])
    )
    g_y = (
        y * (g[1][1] - g[0][0] - g[2][2])
        + x * (g[0][1] + g[1][0])
        + z * (g[1][2] + g[2][1])
        + w * (g[0][2] - g[2][0])
    )
    g_z = (
        z * (g[2][2] - g[0][0] - g[1][1])
        + x * (g[0][2] + g[2][0])
        + y * (g[1][2] + g[2][1])
        + w * (g[1][0] - g[0][1])
    )
    twice = 2.0 * inverse
    return [twice * (g_w - w * along), twice * (g_x - x * along), twice * (g_y - y * along), twice * (g_z - z * along)]


def adam(param, gradient, mean, square, first):
    fixes = [(1.0 - BETA_ONE ** (START + 1 + i), 1.0 - BETA_TWO ** (START + 1 + i)) for i in range(ITERS)]
    fix_one = jnp.where(first, F32(fixes[0][0]), F32(fixes[1][0]))
    fix_two = jnp.where(first, F32(fixes[0][1]), F32(fixes[1][1]))
    mean = BETA_ONE * mean + (1.0 - BETA_ONE) * gradient
    square = BETA_TWO * square + (1.0 - BETA_TWO) * gradient * gradient
    param = param - LEARN_RATE * (mean / fix_one) / (jnp.sqrt(square / fix_two) + EPSILON)
    return param, mean, square


def kernel(
    regions, lanes, own, pairs,
    logd_in, cam_in, pose_in, dmean_in, dsq_in, cmean_in, csq_in, pmean_in, psq_in, points_in, conf_in, images_in, flag_in,
    logd_out, cam_out, pose_out, dmean_out, dsq_out, cmean_out, csq_out, pmean_out, psq_out,
    logd, dmean, dsq, cam, cmean, csq, pose, pmean, psq, points, conf, xs, cw,
    index_rows, gather_hot, scatter_hot, answer_hot, return_hot,
    table, small_table, rows_d, rows_c, rows_g, rows_s, pair_s, wide, narrow, grad_d,
    req_out, req_in, ans_out, ans_in, ret_out, ret_in, edge_d, edge_c, back_d, back_c, part_d, part_c,
    load_sem, send_sem, recv_sem, small_send, small_recv,
):
    share = own // lanes
    slots = CAP * regions
    pair_rows = xs.shape[1]
    pair_lanes = pose.shape[1]
    keys = table.shape[1]
    edge_at = own
    slot_at = own + 16
    region = lax.axis_index("region")
    lane = lax.axis_index("pair")
    my_rows = pl.multiple_of(lane * share, share)

    def ahead(j):
        return lax.rem(region + j, regions)

    def behind(j):
        return lax.rem(region - j + regions, regions)

    def lane_at(k):
        return lax.rem(lane + k, lanes)

    barrier = pltpu.get_barrier_semaphore()

    def greet(j, carry):
        pl.semaphore_signal(barrier, inc=1, device_id={"region": ahead(j)})
        return carry

    lax.fori_loop(1, regions, greet, 0)
    for k in range(1, lanes):
        pl.semaphore_signal(barrier, inc=1, device_id={"pair": lane_at(k)})

    loads = [
        pltpu.make_async_copy(points_in, points, load_sem.at[0]),
        pltpu.make_async_copy(conf_in, conf, load_sem.at[1]),
        pltpu.make_async_copy(dmean_in.at[pl.ds(my_rows, share)], dmean, load_sem.at[2]),
        pltpu.make_async_copy(dsq_in.at[pl.ds(my_rows, share)], dsq, load_sem.at[3]),
        pltpu.make_async_copy(logd_in, logd.at[0], load_sem.at[4]),
    ]
    for load in loads:
        load.start()

    lane_ids = lax.broadcasted_iota(jnp.int32, (1, pair_lanes), 1)
    index_rows[...] = jnp.zeros_like(index_rows)
    index_rows[0:1, 0:pairs] = images_in[0:1, :]
    index_rows[1:2, 0:pairs] = images_in[1:2, :]
    index_rows[2:3, 0:pairs] = flag_in[...]
    real = lane_ids < pairs
    seconds = index_rows[1:2, :]
    remote = jnp.logical_and(index_rows[2:3, :] == 1, real)
    firsts = jnp.where(real, index_rows[0:1, :] - region * own, 0)
    target = lax.div(seconds, jnp.full_like(seconds, own))
    local = seconds - target * own
    offset = target - region
    offset = jnp.where(offset < 0, offset + regions, offset)
    offset = jnp.where(remote, offset, 0)
    offset_column = jnp.transpose(jnp.broadcast_to(offset.astype(F32), (128, pair_lanes)))[:, 0:1]
    earlier_ids = lax.broadcasted_iota(jnp.int32, (pair_lanes, pair_lanes), 0)
    later_ids = lax.broadcasted_iota(jnp.int32, (pair_lanes, pair_lanes), 1)
    same = jnp.logical_and(offset_column == offset.astype(F32), earlier_ids < later_ids)
    rank = jnp.sum(jnp.where(same, 1.0, 0.0), axis=0, keepdims=True).astype(jnp.int32)
    slot = rank * regions + offset - 1
    slot = jnp.where(remote, slot, -1)
    near = jnp.where(target == region, local, edge_at + local)
    near = jnp.where(real, near, 0)
    second_row = jnp.where(remote, slot_at + slot, near)
    wanted = jnp.sum(
        jnp.where(lax.broadcasted_iota(jnp.int32, (slots, pair_lanes), 0) == slot, local.astype(F32), 0.0),
        axis=1,
        keepdims=True,
    )
    half = lax.broadcasted_iota(jnp.int32, (regions, 128), 1) < 64
    request = jnp.where(half, wanted[0:regions], wanted[regions:slots])
    req_out[...] = jnp.broadcast_to(request[:, None, :], req_out.shape)
    req_in[regions - 1] = jnp.full(req_in.shape[1:], -1.0, F32)

    pl.semaphore_wait(barrier, regions - 1 + lanes - 1)

    def ask(j, carry):
        pltpu.make_async_remote_copy(
            src_ref=req_out.at[j - 1],
            dst_ref=req_in.at[j - 1],
            send_sem=small_send.at[0],
            recv_sem=small_recv.at[0],
            device_id={"region": ahead(j)},
        ).start()
        return carry

    lax.fori_loop(1, regions, ask, 0)

    for s, row in enumerate((firsts, second_row)):
        column = jnp.transpose(jnp.broadcast_to(row.astype(F32), (128, pair_lanes)))[0:pair_rows, 0:1]
        key_ids = lax.broadcasted_iota(jnp.int32, (pair_rows, keys), 1).astype(F32)
        gather_hot[s] = jnp.where(column == key_ids, 1.0, 0.0).astype(BF16)
        row_ids = lax.broadcasted_iota(jnp.int32, (keys, pair_lanes), 0)
        scatter_hot[:, s * pair_lanes : (s + 1) * pair_lanes] = jnp.where(row_ids == row, 1.0, 0.0).astype(BF16)

    ones = jnp.ones((8, cam.shape[1]), F32)
    cam[...] = ones
    cmean[...] = ones
    csq[...] = ones
    cam[:, 0:own] = cam_in[...]
    cmean[:, 0:own] = cmean_in[...]
    csq[:, 0:own] = csq_in[...]
    ones = jnp.ones((8, pair_lanes), F32)
    pose[...] = ones
    pmean[...] = ones
    psq[...] = ones
    pose[:, 0:pairs] = pose_in[...]
    pmean[:, 0:pairs] = pmean_in[...]
    psq[:, 0:pairs] = psq_in[...]
    wide[...] = jnp.zeros_like(wide)
    narrow[...] = jnp.zeros_like(narrow)
    rows_g[...] = jnp.zeros_like(rows_g)
    rows_s[...] = jnp.zeros_like(rows_s)
    pair_s[...] = jnp.zeros_like(pair_s)
    table[...] = jnp.zeros_like(table)
    small_table[...] = jnp.zeros_like(small_table)
    loads[4].wait()
    loads[0].wait()
    loads[1].wait()

    weight_row = jnp.where(real, 2.0 * (1.0 + index_rows[2:3, :].astype(F32)), 0.0)
    weight = jnp.transpose(jnp.broadcast_to(weight_row, (128, pair_lanes)))[0:pairs, 0:1]

    def convert(c, carry):
        xs[c, 0:pairs, :] = points[c].astype(F32)
        return carry

    if pair_rows > pairs:
        xs[:, pair_rows - 8 : pair_rows, :] = jnp.zeros((6, 8, ANCH), F32)
        cw[:, pair_rows - 8 : pair_rows, :] = jnp.zeros((2, 8, ANCH), F32)
    lax.fori_loop(0, 6, convert, 0)
    for s in range(2):
        cw[s, 0:pairs, :] = conf[s].astype(F32) * weight

    anchor = lax.broadcasted_iota(jnp.int32, (8, 128), 1)
    across = (8 * lax.rem(anchor, jnp.full_like(anchor, ANCH_W)) + 4 - 4 * ANCH_W).astype(F32)
    downward = (8 * lax.div(anchor, jnp.full_like(anchor, ANCH_W)) + 4 - 4 * ANCH_H).astype(F32)
    down_step = 8.0 * (128 // ANCH_W)
    column_ids = lax.broadcasted_iota(jnp.int32, (8, 128), 1)

    def wait_small(sem, which, count):
        pltpu.make_async_copy(req_in.at[pl.ds(0, count)], req_in.at[pl.ds(0, count)], sem.at[which]).wait()

    def wait_messages(sem, which):
        whole = ans_in.at[0, pl.ds(0, MSG * (regions - 1))]
        pltpu.make_async_copy(whole, whole, sem.at[which]).wait()

    wait_small(small_recv, 0, regions - 1)
    asked = req_in[:, 0, :]
    ids = lax.broadcasted_iota(jnp.int32, (regions, own), 1).astype(F32)
    for c in range(CAP):
        hot = jnp.where(asked[:, 64 * c : 64 * c + 1] == ids, 1.0, 0.0)
        answer_hot[c * regions : (c + 1) * regions, :] = hot.astype(BF16)
    asked_rows = jnp.transpose(jnp.concatenate([asked, asked], 0)) if regions == 64 else None
    if regions == 64:
        both = jnp.concatenate([asked_rows[0:1, 0:64], asked_rows[64:65, 0:64]], 1)
        row_ids = lax.broadcasted_iota(jnp.int32, (own, slots), 0).astype(F32)
        return_hot[...] = jnp.where(row_ids == both, 1.0, 0.0).astype(BF16)
    else:
        return_hot[...] = jnp.transpose(answer_hot[...].astype(F32)).astype(BF16)

    def send_messages(it, phase, src, dst, towards):
        def send(j, carry):
            at = pl.ds(pl.multiple_of((j - 1) * MSG, MSG), MSG)
            pltpu.make_async_remote_copy(
                src_ref=src.at[it, at],
                dst_ref=dst.at[it, at],
                send_sem=send_sem.at[2 * it + phase],
                recv_sem=recv_sem.at[2 * it + phase],
                device_id={"region": towards(j)},
            ).start()
            return carry

        lax.fori_loop(1, regions, send, 0)

    def pack(dst, it, depths, smalls):
        for c in range(CAP):
            for g in range(regions // 8):
                rows = slice(c * regions + 8 * g, c * regions + 8 * g + 8)
                for t in range(TILES):
                    at = MSG * 8 * g + TILES * c + t
                    dst[it, pl.ds(at, 8, stride=MSG), :] = depths[rows, 128 * t : 128 * t + 128]
        for g in range(regions // 8):
            low = smalls[8 * g : 8 * g + 8, :]
            high = smalls[regions + 8 * g : regions + 8 * g + 8, :]
            dst[it, pl.ds(MSG * 8 * g + CAP * TILES, 8, stride=MSG), :] = low + pltpu.roll(high, 64, 1)

    def unpack_depths(src, it, c, g, t):
        return src[it, pl.ds(MSG * 8 * g + TILES * c + t, 8, stride=MSG), :]

    def unpack_smalls(src, it, c, g):
        value = src[it, pl.ds(MSG * 8 * g + CAP * TILES, 8, stride=MSG), :]
        value = jnp.where(column_ids < 64, value, 0.0) if c == 0 else jnp.where(column_ids < 64, pltpu.roll(value, 64, 1), 0.0)
        return value

    def small_copy(it, phase, src, dst, device_id):
        return pltpu.make_async_remote_copy(
            src_ref=src,
            dst_ref=dst,
            send_sem=small_send.at[1 + 16 * it + phase],
            recv_sem=small_recv.at[1 + 16 * it + phase],
            device_id=device_id,
        )

    def iteration(it, carry):
        first = it == 0
        q = [cam[k : k + 1, :] for k in range(4)]
        turn, turn_inverse = rotation_rows(*q)
        near_focal = jnp.exp(-cam[7:8, :])
        for k in range(3):
            narrow[4 * k : 4 * k + 1, :] = turn[k][0] * near_focal
            narrow[4 * k + 1 : 4 * k + 2, :] = turn[k][1] * near_focal
            narrow[4 * k + 2 : 4 * k + 3, :] = turn[k][2]
            narrow[4 * k + 3 : 4 * k + 4, :] = cam[4 + k : 5 + k, :]
        coefs = jnp.transpose(narrow[...])[0:own, :]
        small_table[0:own, :] = coefs
        depth = jnp.exp(logd[it])
        edge_d[it, 0] = depth[0:EDGE, :]
        edge_c[it, 0] = coefs[0:EDGE, :]
        edge_copies = [
            small_copy(it, 0, edge_d.at[it, 0], edge_d.at[it, 1], {"region": behind(1)}),
            small_copy(it, 1, edge_c.at[it, 0], edge_c.at[it, 1], {"region": behind(1)}),
        ]
        for copy in edge_copies:
            copy.start()
        pieces = split_three(depth)
        for n in range(3):
            table[n, 0:own, :] = pieces[n]
        answer = dot(answer_hot[...], pieces[0]) + (dot(answer_hot[...], pieces[1]) + dot(answer_hot[...], pieces[2]))
        pack(ans_out, it, answer, dot_exact(answer_hot[...], coefs))
        send_messages(it, 0, ans_out, ans_in, behind)

        p = [pose[k : k + 1, :] for k in range(4)]
        bend, bend_inverse = rotation_rows(*p)
        scale = jnp.exp(pose[7:8, :])
        for k in range(3):
            for j in range(3):
                wide[4 * k + j : 4 * k + j + 1, :] = scale * bend[k][j]
            wide[4 * k + 3 : 4 * k + 4, :] = scale * pose[4 + k : 5 + k, :]
        rows_p = jnp.transpose(wide[...])
        rows_s[1, 0:pair_lanes, :] = rows_p

        for copy in edge_copies:
            copy.wait_recv()
        pieces = split_three(jnp.concatenate([edge_d[it, 1], jnp.zeros((8, ANCH), F32)], 0))
        for n in range(3):
            table[n, edge_at : edge_at + 16, :] = pieces[n]
        small_table[edge_at : edge_at + EDGE, :] = edge_c[it, 1]
        wait_messages(recv_sem, 2 * it)
        ans_in[it, MSG * (regions - 1) : MSG * regions, :] = jnp.zeros((MSG, 128), F32)
        for c in range(CAP):
            for g in range(0, regions // 8, 2):
                at = slot_at + c * regions + 8 * g
                for t in range(TILES):
                    value = jnp.concatenate(
                        [unpack_depths(ans_in, it, c, g, t), unpack_depths(ans_in, it, c, g + 1, t)], 0
                    )
                    pieces = split_three(value)
                    for n in range(3):
                        table[n, at : at + 16, 128 * t : 128 * t + 128] = pieces[n]
                small_table[at : at + 8, :] = unpack_smalls(ans_in, it, c, g)
                small_table[at + 8 : at + 16, :] = unpack_smalls(ans_in, it, c, g + 1)

        for s in range(2):
            for n in range(0, ANCH, 256):
                part = slice(n, n + 256)
                rows_d[s, :, part] = dot(gather_hot[s], table[0, :, part]) + (
                    dot(gather_hot[s], table[1, :, part]) + dot(gather_hot[s], table[2, :, part])
                )
            rows_c[s] = dot_exact(gather_hot[s], small_table[...])

        def group(g, inner):
            at = pl.ds(pl.multiple_of(g * 8, 8), 8)
            pose_values = rows_s[1, at, :]

            def spread(values, c):
                return jnp.broadcast_to(values[:, c : c + 1], (8, 128))

            shift = [[spread(pose_values, 4 * k + j) for j in range(4)] for k in range(3)]
            turned = [[jnp.zeros((8, 128), F32) for j in range(3)] for k in range(3)]
            moved = [jnp.zeros((8, 128), F32) for k in range(3)]
            for s in range(2):
                camera = rows_c[s, at, :]
                ray = []
                step = []
                place = []
                for k in range(3):
                    down = spread(camera, 4 * k + 1)
                    ray.append(spread(camera, 4 * k) * across + (down * downward + spread(camera, 4 * k + 2)))
                    step.append(down * down_step)
                    place.append(spread(camera, 4 * k + 3))
                total = [jnp.zeros((8, 128), F32) for k in range(3)]
                by_depth = [jnp.zeros((8, 128), F32) for k in range(3)]
                by_down = [jnp.zeros((8, 128), F32) for k in range(3)]
                for t in range(TILES):
                    part = slice(128 * t, 128 * t + 128)
                    d = rows_d[s, at, part]
                    c = cw[s, at, part]
                    x = [xs[3 * s + j, at, part] for j in range(3)]
                    along = None
                    for k in range(3):
                        placed = shift[k][0] * x[0] + shift[k][1] * x[1] + (shift[k][2] * x[2] + shift[k][3])
                        pull = c * ((d * ray[k] + place[k]) - placed)
                        for j in range(3):
                            turned[k][j] = turned[k][j] + pull * x[j]
                        total[k] = total[k] + pull
                        deep = pull * d
                        by_depth[k] = by_depth[k] + deep
                        if t > 0:
                            by_down[k] = by_down[k] + F32(t) * deep
                        along = deep * ray[k] if along is None else along + deep * ray[k]
                        if t < TILES - 1:
                            ray[k] = ray[k] + step[k]
                    rows_g[pl.ds(pl.multiple_of(s * pair_lanes + g * 8, 8), 8), part] = along
                out = jnp.zeros((8, 128), F32)
                for k in range(3):
                    moved[k] = moved[k] + total[k]
                    values = [
                        by_depth[k] * across,
                        by_depth[k] * downward + by_down[k] * down_step,
                        by_depth[k],
                        total[k],
                    ]
                    for j in range(4):
                        out = jnp.where(column_ids == 4 * k + j, jnp.sum(values[j], axis=1, keepdims=True), out)
                rows_s[0, pl.ds(pl.multiple_of(s * pair_lanes + g * 8, 8), 8), :] = out
            out = jnp.zeros((8, 128), F32)
            for k in range(3):
                for j in range(3):
                    out = jnp.where(column_ids == 4 * k + j, jnp.sum(turned[k][j], axis=1, keepdims=True), out)
                out = jnp.where(column_ids == 4 * k + 3, jnp.sum(moved[k], axis=1, keepdims=True), out)
            pair_s[at, :] = out
            return inner

        lax.fori_loop(0, pair_rows // 8, group, 0)

        last = rounded(slot_at + slots, 16)
        hot = scatter_hot[0:last, :]
        for n in range(0, ANCH, 256):
            part = slice(n, n + 256)
            high, low = split_two(rows_g[:, part])
            grad_d[:, part] = dot(hot, high) + dot(hot, low)
        sums = dot_exact(hot, rows_s[0])
        pack(ret_out, it, grad_d[slot_at : slot_at + slots, :], sums[slot_at : slot_at + slots, :])
        send_messages(it, 1, ret_out, ret_in, ahead)
        back_d[it, 0] = grad_d[edge_at : edge_at + EDGE, :]
        back_c[it, 0] = sums[edge_at : edge_at + EDGE, :]
        back_copies = [
            small_copy(it, 2, back_d.at[it, 0], back_d.at[it, 1], {"region": ahead(1)}),
            small_copy(it, 3, back_c.at[it, 0], back_c.at[it, 1], {"region": ahead(1)}),
        ]
        for copy in back_copies:
            copy.start()

        found = jnp.transpose(pair_s[...])
        m = [[found[4 * k + j : 4 * k + j + 1, :] for j in range(3)] for k in range(3)]
        v = [found[4 * k + 3 : 4 * k + 4, :] for k in range(3)]
        g_turn = [[-(scale * m[k][j]) for j in range(3)] for k in range(3)]
        g_pose = rotation_pull(p, bend, bend_inverse, g_turn)
        g_scale = sum(bend[k][j] * g_turn[k][j] for k in range(3) for j in range(3))
        for k in range(3):
            g_move = -(scale * v[k])
            g_scale = g_scale + pose[4 + k : 5 + k, :] * g_move
            g_pose.append(g_move)
        g_pose.append(g_scale)
        for k in range(8):
            row = slice(k, k + 1)
            pose[row, :], pmean[row, :], psq[row, :] = adam(pose[row, :], g_pose[k], pmean[row, :], psq[row, :], first)

        wait_messages(recv_sem, 2 * it + 1)
        for copy in back_copies:
            copy.wait_recv()
        ret_in[it, MSG * (regions - 1) : MSG * regions, :] = jnp.zeros((MSG, 128), F32)
        hot = return_hot[...]
        for t in range(TILES):
            part = slice(128 * t, 128 * t + 128)
            value = jnp.concatenate(
                [unpack_depths(ret_in, it, c, g, t) for c in range(CAP) for g in range(regions // 8)], 0
            )
            high, low = split_two(value)
            grad_d[0:own, part] = grad_d[0:own, part] + (dot(hot, high) + dot(hot, low))
        grad_d[0:EDGE, :] = grad_d[0:EDGE, :] + back_d[it, 1]
        value = jnp.concatenate([unpack_smalls(ret_in, it, c, g) for c in range(CAP) for g in range(regions // 8)], 0)
        sums = sums[0:own, :] + dot_exact(hot, value)
        sums = jnp.concatenate([sums[0:EDGE, :] + back_c[it, 1], sums[EDGE:own, :]], 0)
        if own < 128:
            sums = jnp.concatenate([sums, jnp.zeros((128 - own, 128), F32)], 0)
        part_c[it, lane] = jnp.transpose(sums)[0:16, :]

        lane_copies = []
        for k in range(1, lanes):
            to = lane_at(k)
            rows = pl.ds(pl.multiple_of(to * share, share), share)
            lane_copies.append(small_copy(it, 4 + k, grad_d.at[rows], part_d.at[it, k - 1], {"pair": to}))
            lane_copies.append(small_copy(it, 7 + k, part_c.at[it, lane], part_c.at[it, lane], {"pair": to}))
        for copy in lane_copies:
            copy.start()
        for copy in lane_copies:
            copy.wait_recv()
        gradient = grad_d[pl.ds(my_rows, share), :]
        for k in range(1, lanes):
            gradient = gradient + part_d[it, k - 1]
        updated, dmean[...], dsq[...] = adam(logd[it, pl.ds(my_rows, share), :], gradient, dmean[...], dsq[...], first)
        logd[it + 1, pl.ds(my_rows, share), :] = updated
        mine = logd.at[it + 1, pl.ds(my_rows, share)]
        gathers = [small_copy(it, 10 + k, mine, mine, {"pair": lane_at(k)}) for k in range(1, lanes)]
        for copy in gathers:
            copy.start()

        found = part_c[it, 0]
        for k in range(1, lanes):
            found = found + part_c[it, k]
        across_sum = [found[4 * k : 4 * k + 1, :] * near_focal for k in range(3)]
        down_sum = [found[4 * k + 1 : 4 * k + 2, :] * near_focal for k in range(3)]
        g_turn = [[across_sum[k], down_sum[k], found[4 * k + 2 : 4 * k + 3, :]] for k in range(3)]
        g_cam = rotation_pull(q, turn, turn_inverse, g_turn)
        for k in range(3):
            g_cam.append(found[4 * k + 3 : 4 * k + 4, :])
        g_cam.append(-sum(turn[k][0] * across_sum[k] + turn[k][1] * down_sum[k] for k in range(3)))
        for k in range(8):
            row = slice(k, k + 1)
            cam[row, :], cmean[row, :], csq[row, :] = adam(cam[row, :], g_cam[k], cmean[row, :], csq[row, :], first)
        for copy in lane_copies + edge_copies + back_copies:
            copy.wait_send()
        for copy in gathers:
            copy.wait()
        return carry

    loads[2].wait()
    loads[3].wait()
    lax.fori_loop(0, ITERS, iteration, 0)

    wait_small(small_send, 0, regions - 1)
    for phase in range(2 * ITERS):
        wait_messages(send_sem, phase)
    logd_out[...] = logd[ITERS]
    cam_out[...] = cam[:, 0:own]
    pose_out[...] = pose[:, 0:pairs]
    pmean_out[...] = pmean[:, 0:pairs]
    psq_out[...] = psq[:, 0:pairs]
    dmean_out[...] = dmean[...]
    dsq_out[...] = dsq[...]
    for src, dst in ((cmean, cmean_out), (csq, csq_out)):
        value = src[:, 0:share]
        for k in range(1, lanes):
            value = jnp.where(lane == k, src[:, k * share : (k + 1) * share], value)
        dst[...] = value


def shards(
    log_depth, cameras, pair_pose, depth_mean, depth_square, camera_mean, camera_square, pose_mean, pose_square,
    pointmaps, confidence, pair_images, pair_flag,
):
    regions = lax.axis_size("region")
    lanes = lax.axis_size("pair")
    own = log_depth.shape[0]
    pairs = pair_pose.shape[0]
    share = own // lanes
    slots = CAP * regions
    pair_rows = rounded(pairs, 8)
    pair_lanes = rounded(pairs, 128)
    keys = rounded(own + 16 + slots, 128)
    last = rounded(own + 16 + slots, 16)
    in_vmem = pl.BlockSpec(memory_space=pltpu.VMEM)
    anywhere = pl.BlockSpec(memory_space=pl.ANY)

    def vmem(*shape, dtype=F32):
        return pltpu.VMEM(shape, dtype)

    def out(*shape):
        return jax.ShapeDtypeStruct(shape, F32)

    results = pl.pallas_call(
        functools.partial(kernel, regions, lanes, own, pairs),
        out_shape=(
            out(own, ANCH), out(8, own), out(8, pairs), out(share, ANCH), out(share, ANCH),
            out(8, share), out(8, share), out(8, pairs), out(8, pairs),
        ),
        in_specs=[
            anywhere, in_vmem, in_vmem, anywhere, anywhere, in_vmem, in_vmem, in_vmem, in_vmem,
            anywhere, anywhere, in_vmem, in_vmem,
        ],
        out_specs=(in_vmem,) * 9,
        scratch_shapes=[
            vmem(ITERS + 1, own, ANCH), vmem(share, ANCH), vmem(share, ANCH),
            vmem(8, 128), vmem(8, 128), vmem(8, 128),
            vmem(8, pair_lanes), vmem(8, pair_lanes), vmem(8, pair_lanes),
            vmem(6, pairs, ANCH, dtype=BF16), vmem(2, pairs, ANCH, dtype=BF16),
            vmem(6, pair_rows, ANCH), vmem(2, pair_rows, ANCH),
            vmem(8, pair_lanes, dtype=jnp.int32),
            vmem(2, pair_rows, keys, dtype=BF16), vmem(keys, 2 * pair_lanes, dtype=BF16),
            vmem(slots, own, dtype=BF16), vmem(own, slots, dtype=BF16),
            vmem(3, keys, ANCH, dtype=BF16), vmem(keys, 128),
            vmem(2, pair_rows, ANCH), vmem(2, pair_rows, 128),
            vmem(2 * pair_lanes, ANCH), vmem(2, 2 * pair_lanes, 128), vmem(pair_lanes, 128),
            vmem(128, pair_lanes), vmem(128, 128), vmem(last, ANCH),
            vmem(regions, 8, 128), vmem(regions, 8, 128),
            vmem(ITERS, MSG * regions, 128), vmem(ITERS, MSG * regions, 128),
            vmem(ITERS, MSG * regions, 128), vmem(ITERS, MSG * regions, 128),
            vmem(ITERS, 2, EDGE, ANCH), vmem(ITERS, 2, EDGE, 128),
            vmem(ITERS, 2, EDGE, ANCH), vmem(ITERS, 2, EDGE, 128),
            vmem(ITERS, lanes - 1, share, ANCH), vmem(ITERS, lanes, 16, 128),
            pltpu.SemaphoreType.DMA((5,)),
            pltpu.SemaphoreType.DMA((2 * ITERS,)), pltpu.SemaphoreType.DMA((2 * ITERS,)),
            pltpu.SemaphoreType.DMA((1 + 16 * ITERS,)), pltpu.SemaphoreType.DMA((1 + 16 * ITERS,)),
        ],
        compiler_params=pltpu.CompilerParams(
            collective_id=0, has_side_effects=True, vmem_limit_bytes=48 * 1024 * 1024
        ),
        name="align",
    )(
        log_depth, cameras.T, pair_pose.T, depth_mean, depth_square, camera_mean.T, camera_square.T,
        pose_mean.T, pose_square.T, pointmaps.transpose(1, 0, 2), confidence.transpose(1, 0, 2),
        pair_images.T, pair_flag.reshape(1, pairs),
    )
    depth, camera, pose, dmean, dsq, cmean, csq, pmean, psq = results
    return depth, camera.T, pose.T, dmean, dsq, cmean.T, csq.T, pmean.T, psq.T


def solution(mesh):
    placed = (
        P("region", None),
        P("region", None),
        P(("region", "pair"), None),
        P("region", None),
        P("region", None),
        P("region", None),
        P("region", None),
        P(("region", "pair"), None),
        P(("region", "pair"), None),
        P(("region", "pair"), None, None),
        P(("region", "pair"), None, None),
        P(("region", "pair"), None),
        P(("region", "pair")),
    )
    return jax.shard_map(
        shards,
        mesh=mesh,
        in_specs=placed,
        out_specs=(
            P("region", None),
            P("region", None),
            P(("region", "pair"), None),
            P(("region", "pair"), None),
            P(("region", "pair"), None),
            P(("region", "pair"), None),
            P(("region", "pair"), None),
            P(("region", "pair"), None),
            P(("region", "pair"), None),
        ),
        check_vma=False,
    )
```

time: 484 us -> 136 us (0.28); the launches traced: 475 us -> 135 us
  waiting for transfers between devices: 164 us -> 0 us
  local copies, waits for them, and re-layouts: 150 us -> 16.4 us
  Pallas kernels: 0 us -> 118 us
  other arithmetic: 69.6 us -> 0 us
  starting transfers between devices: 47.4 us -> 0 us
  blocking collectives: 16.9 us -> 0 us
  between operations: 17 us -> 0.68 us
  matrix products: 9.93 us -> 0 us
    pallas_call x0 -> x1, Pallas kernels: none -> 118 us  [shards(): pl.pallas_call(functools.partial(kernel, regions, lanes, own, pairs), out...]
    psum x2 -> x0, waiting for transfers between devices: 78 us -> none  [shards(): grad_depth, grad_camera = lax.psum((grad_depth, grad_camera), 'pair')]
    all_to_all x5 -> x0, waiting for transfers between devices: 72.1 us -> none  [the longest x2 38.3 us: shards(): lax.all_to_all(outgoing.reshape(regions, capacity, 3, ANCH), 'region', sp...]
    scatter x3 -> x0, local copies, waits for them, and re-layouts: 44.4 us -> none  [the longest x2 43.3 us: shards(): jnp.zeros((slot_total, 3, ANCH), jnp.float32).at[slot_index]]
    gather x8 -> x0, local copies, waits for them, and re-layouts: 33.9 us -> none  [the longest x2 9.9 us: shards(): answers[safe_slot]]
    all_to_all x5 -> x0, starting transfers between devices: 32.1 us -> none  [the longest x2 14 us: shards(): lax.all_to_all(outgoing.reshape(regions, capacity, 3, ANCH), 'region', sp...]
    another operation x13 -> x0, local copies, waits for them, and re-layouts: 19.4 us -> none  [the longest x8 16.3 us: pair_loss(): placed = jnp.stack([chi_first, chi_second], 1)]
    psum x2 -> x0, blocking collectives: 16.9 us -> none  [shards(): grad_depth, grad_camera = lax.psum((grad_depth, grad_camera), 'pair')]
  transfers between devices with their start and end apart: 15 -> 0, of which waited for: 10 -> 0; matrix products, arithmetic and copies ran while one was open for 15% -> 0% of each run, Pallas kernels for 0% -> 0%
where the time goes in v1:
time: 136 us; the launch traced here: 135 us
  Pallas kernels  118 us (87%)
  local copies, waits for them, and re-layouts  16.4 us (12%)
    pallas_call x1, Pallas kernels, shards(): pl.pallas_call(functools.partial(kernel, regions, lanes, own, pairs), out...  118 us
    unnamed x34, local copies, waits for them, and re-layouts  16.4 us

profile of v1, /device:TPU:4, one launch (start us, length us, event | category | flops | bytes accessed | tf_op | source)
XLA Modules:
  0.0 135.3 jit_solution(13211996561190918999)
XLA Ops:
  0.6 1.1 copy.24
  1.8 0.0 copy-start
  1.8 1.5 %copy-done = bf16[190,6,768]{2,0,1:T(8,128)(2,1)S(1)} copy-done((bf16[190,6,768]{2,0,1:T(8,128)(2,1)S(1)}, bf16[190,6,768]{2,0,1:T(8,128)(2,1)}, u32[]{:S(2)}) %copy-start) | copy-done | bytes 1751064
  3.2 0.9 copy-done.1
  4.2 0.9 copy-done.2
  5.1 0.9 copy-done.3
  6.0 0.7 copy-done.4
  6.7 0.7 copy-done.5
  7.4 0.7 copy-done.6
  8.1 0.7 copy-done.7
  8.8 0.7 copy-done.8
  9.5 0.7 copy-done.9
  10.2 0.7 copy-done.10
  10.9 0.7 copy-done.11
  11.5 118.2 %align.1 = (f32[64,768]{1,0:T(8,128)S(1)}, f32[8,64]{1,0:T(8,128)S(1)}, f32[8,190]{1,0:T(8,128)S(1)}, f32[16,768]{1,0:T(8,128)S(1)}, f32[16,768]{1,0:T(8,128)S(1...) custom-call(f32[64,768]{1,0:T(8,128)S(1)} %copy-done.1, ...), custom_call_target="tpu_custom_call" | custom-call | tf_op jit(solution)/shard_map/align/pallas_call | solution.py:584
  129.8 0.7 copy.34
  130.5 0.6 copy.35
  131.1 0.6 copy.36
  131.7 0.6 copy.37
  132.3 0.6 copy.38
  132.9 0.6 copy.39
  133.5 0.6 copy.40
  134.1 0.6 copy.41
  134.7 0.6 copy.42
  (11 shorter events, 0.0 us)
Async XLA Ops:
  1.8 1.5 %copy-start = (bf16[190,6,768]{2,0,1:T(8,128)(2,1)S(1)}, bf16[190,6,768]{2,0,1:T(8,128)(2,1)}, u32[]{:S(2)}) copy-start(bf16[190,6,768]{2,0,1:T(8,128)(2,1)} %param.22) | copy-start | bytes 5253124
  3.2 0.9 copy-start.1
  4.2 0.9 copy-start.2
  5.1 0.9 copy-start.3
  6.0 0.7 copy-start.4
  6.7 0.7 copy-start.5
  7.4 0.7 copy-start.6
  8.1 0.7 copy-start.7
  8.8 0.7 copy-start.8
  9.5 0.7 copy-start.9
  10.2 0.7 copy-start.10
  10.9 0.7 copy-start.11

commit v2 on v1

v2 whole, which is shorter than its diff:
```python
import functools

import jax
import jax.numpy as jnp
from jax import lax
from jax.experimental import pallas as pl
from jax.experimental.pallas import tpu as pltpu
from jax.sharding import PartitionSpec as P

ANCH_W = 32
ANCH_H = 24
ANCH = 768
CAP = 2
NEIGHBOURS = 4
ITERS = 2
START = 300

LEARN_RATE = 0.01
BETA_ONE = 0.9
BETA_TWO = 0.999
EPSILON = 1e-08

TILES = ANCH // 128
EDGE = 8
MAPS = 4
MSG = TILES * CAP * MAPS
CHUNKS = 3
COEFS = 16
F32 = jnp.float32
BF16 = jnp.bfloat16


def rounded(value, multiple):
    return -(-value // multiple) * multiple


def split_two(x):
    high = x.astype(BF16)
    return high, (x - high.astype(F32)).astype(BF16)


def split_three(x):
    high = x.astype(BF16)
    rest = x - high.astype(F32)
    middle = rest.astype(BF16)
    return high, middle, (rest - middle.astype(F32)).astype(BF16)


def dot(a, b):
    return jnp.dot(a, b, preferred_element_type=F32)


def dot_exact(one_hot, x):
    high, middle, low = split_three(x)
    return dot(one_hot, high) + (dot(one_hot, middle) + dot(one_hot, low))


def pack_three(x):
    high, middle, low = split_three(x)
    rest = pltpu.roll(middle.astype(F32), COEFS, 1) + pltpu.roll(low.astype(F32), 2 * COEFS, 1)
    return (high.astype(F32) + rest).astype(BF16)


def rotation_rows(w, x, y, z):
    inverse = 1.0 / (w * w + x * x + y * y + z * z)
    matrix = [
        [w * w + x * x - y * y - z * z, 2.0 * (x * y - w * z), 2.0 * (x * z + w * y)],
        [2.0 * (x * y + w * z), w * w - x * x + y * y - z * z, 2.0 * (y * z - w * x)],
        [2.0 * (x * z - w * y), 2.0 * (y * z + w * x), w * w - x * x - y * y + z * z],
    ]
    return [[entry * inverse for entry in line] for line in matrix], inverse


def rotation_pull(q, matrix, inverse, g):
    w, x, y, z = q
    along = sum(g[k][j] * matrix[k][j] for k in range(3) for j in range(3))
    diag = g[0][0] + g[1][1] + g[2][2]
    g_w = w * diag + z * (g[1][0] - g[0][1]) + y * (g[0][2] - g[2][0]) + x * (g[2][1] - g[1][2])
    g_x = (
        x * (g[0][0] - g[1][1] - g[2][2])
        + y * (g[0][1] + g[1][0])
        + z * (g[0][2] + g[2][0])
        + w * (g[2][1] - g[1][2])
    )
    g_y = (
        y * (g[1][1] - g[0][0] - g[2][2])
        + x * (g[0][1] + g[1][0])
        + z * (g[1][2] + g[2][1])
        + w * (g[0][2] - g[2][0])
    )
    g_z = (
        z * (g[2][2] - g[0][0] - g[1][1])
        + x * (g[0][2] + g[2][0])
        + y * (g[1][2] + g[2][1])
        + w * (g[1][0] - g[0][1])
    )
    twice = 2.0 * inverse
    return [twice * (g_w - w * along), twice * (g_x - x * along), twice * (g_y - y * along), twice * (g_z - z * along)]


def adam(param, gradient, mean, square, first):
    fixes = [(1.0 - BETA_ONE ** (START + 1 + i), 1.0 - BETA_TWO ** (START + 1 + i)) for i in range(ITERS)]
    fix_one = jnp.where(first, F32(fixes[0][0]), F32(fixes[1][0]))
    fix_two = jnp.where(first, F32(fixes[0][1]), F32(fixes[1][1]))
    mean = BETA_ONE * mean + (1.0 - BETA_ONE) * gradient
    square = BETA_TWO * square + (1.0 - BETA_TWO) * gradient * gradient
    param = param - LEARN_RATE * (mean / fix_one) / (jnp.sqrt(square / fix_two) + EPSILON)
    return param, mean, square


def kernel(
    regions, lanes, own, pairs,
    logd_hbm, cam_hbm, pose_hbm, dmean_hbm, dsq_hbm, cmean_hbm, csq_hbm, pmean_hbm, psq_hbm, points_hbm, conf_hbm,
    images_hbm, flag_hbm,
    logd_out, cam_out, pose_out, dmean_out, dsq_out, cmean_out, csq_out, pmean_out, psq_out,
    cam_in, cmean_in, csq_in, pose_in, pmean_in, psq_in, images_in, flag_in,
    logd, dmean, dsq, cam, cmean, csq, pose, pmean, psq, points, conf, xs, cw,
    index_rows, pick_hot, back_hot, gather_hot, scatter_hot, camera_ones, pose_ones,
    table, small_table, rows_d, rows_c, rows_p, rows_g, rows_s, wide, narrow, grad_d, grad_s,
    small_out, small_in, bulk_out, bulk_in, first_out, first_in, second_out, second_in,
    edge_d, edge_c, back_d, back_c, part_d, part_c, moments,
    load_sem, send_sem, recv_sem, small_send, small_recv,
):
    share = own // lanes
    slots = CAP * regions
    nearby = pairs - CAP * (regions - 1)
    pair_lanes = pose.shape[1] - rounded(slots, 128)
    total_rows = pose.shape[1]
    near_at = pair_lanes - nearby
    keys = own + 16
    region = lax.axis_index("region")
    lane = lax.axis_index("pair")
    my_rows = pl.multiple_of(lane * share, share)

    def ahead(j):
        return lax.rem(region + j, regions)

    def behind(j):
        return lax.rem(region - j + regions, regions)

    def lane_at(k):
        return lax.rem(lane + k, lanes)

    loads = [
        pltpu.make_async_copy(src, dst, load_sem.at[n])
        for n, (src, dst) in enumerate(
            (
                (images_hbm, images_in), (flag_hbm, flag_in), (points_hbm, points), (conf_hbm, conf), (logd_hbm, logd.at[0]),
                (cam_hbm, cam_in), (cmean_hbm, cmean_in), (csq_hbm, csq_in),
                (pose_hbm, pose_in), (pmean_hbm, pmean_in), (psq_hbm, psq_in),
                (dmean_hbm.at[pl.ds(my_rows, share)], dmean), (dsq_hbm.at[pl.ds(my_rows, share)], dsq),
            )
        )
    ]
    for load in loads:
        load.start()

    barrier = pltpu.get_barrier_semaphore()

    def greet(j, carry):
        pl.semaphore_signal(barrier, inc=1, device_id={"region": ahead(j)})
        return carry

    lax.fori_loop(1, regions, greet, 0)
    for k in range(1, lanes):
        pl.semaphore_signal(barrier, inc=1, device_id={"pair": lane_at(k)})

    for load in loads:
        load.wait()

    def as_column(row):
        return jnp.transpose(jnp.broadcast_to(row, (128, row.shape[1])))[:, 0:1]

    lane_ids = lax.broadcasted_iota(jnp.int32, (1, pair_lanes), 1)
    index_rows[...] = jnp.zeros_like(index_rows)
    index_rows[0:2, 0:pairs] = images_in[...]
    index_rows[2:3, 0:pairs] = flag_in[...]
    real = lane_ids < pairs
    seconds = index_rows[1:2, :]
    flags = index_rows[2:3, :]
    remote = jnp.logical_and(flags == 1, real)
    firsts = jnp.where(real, index_rows[0:1, :] - region * own, 0).astype(F32)
    target = lax.div(seconds, jnp.full_like(seconds, own))
    local = seconds - target * own
    offset = target - region
    offset = jnp.where(offset < 0, offset + regions, offset)
    offset = jnp.where(remote, offset, 0).astype(F32)
    near = jnp.where(target == region, local, own + local).astype(F32)
    local = local.astype(F32)
    earlier_ids = lax.broadcasted_iota(jnp.int32, (pair_lanes, pair_lanes), 0)
    later_ids = lax.broadcasted_iota(jnp.int32, (pair_lanes, pair_lanes), 1)
    same = jnp.logical_and(as_column(offset) == offset, earlier_ids < later_ids)
    rank = jnp.sum(jnp.where(same, 1.0, 0.0), axis=0, keepdims=True)
    place = jnp.where(remote, rank * regions + offset - 1.0, slots + rank)
    place = jnp.where(real, place, -1.0)
    place_ids = lax.broadcasted_iota(jnp.int32, pick_hot.shape, 0).astype(F32)
    picked = place_ids == place
    pick_hot[...] = jnp.where(picked, 1.0, 0.0).astype(BF16)
    near = jnp.sum(jnp.where(picked, near, 0.0), axis=1, keepdims=True)[slots : slots + nearby]

    ones = jnp.ones((8, total_rows), F32)
    for padded, values in ((pose, pose_in), (pmean, pmean_in), (psq, psq_in)):
        padded[...] = ones
        padded[:, 0:pairs] = values[...]
    wide[...] = jnp.zeros_like(wide)
    wide[0:8, :] = pose[...]
    wide[8:16, :] = pmean[...]
    wide[16:24, :] = psq[...]
    wide[24:25, 0:pair_lanes] = local
    details = dot_exact(pick_hot[...], jnp.transpose(wide[:, 0:pair_lanes]))[0:slots]
    wide[...] = jnp.zeros_like(wide)

    def halves(values):
        return values[0:regions] + pltpu.roll(values[regions:slots], 64, 1)

    def from_halves(values):
        low = lax.broadcasted_iota(jnp.int32, values.shape, 1) < 64
        return jnp.concatenate([jnp.where(low, values, 0.0), jnp.where(low, pltpu.roll(values, 64, 1), 0.0)], 0)

    small_out[...] = halves(details)
    small_in[regions - 1 : regions, :] = jnp.ones((1, 128), F32)
    weights = 2.0 * (1.0 + flags.astype(F32))
    weights = jnp.where(real, weights, 0.0)
    weight_column = as_column(weights)
    slot_weights = jnp.sum(jnp.where(picked, weights, 0.0), axis=1, keepdims=True)
    xs[...] = jnp.zeros_like(xs)
    cw[...] = jnp.zeros_like(cw)
    for m in range(MAPS):
        source = points[3 + m] if m < 3 else conf[1]
        chosen = dot(pick_hot[:, 0:pairs], source)
        if m == 3:
            chosen = chosen * slot_weights
        for c in range(CAP):
            for g in range(regions // 8):
                rows = slice(c * regions + 8 * g, c * regions + 8 * g + 8)
                for t in range(TILES):
                    at = MSG * 8 * g + CAP * MAPS * t + MAPS * c + m
                    bulk_out[pl.ds(at, 8, stride=MSG), :] = chosen[rows, 128 * t : 128 * t + 128]
        if m < 3:
            xs[m, near_at:pair_lanes, :] = chosen[slots : slots + nearby]
        else:
            cw[near_at:pair_lanes, :] = chosen[slots : slots + nearby]

    def send_row(src, dst, which, j, to):
        at = pl.ds(j - 1, 1)
        pltpu.make_async_remote_copy(
            src_ref=src.at[at],
            dst_ref=dst.at[at],
            send_sem=send_sem.at[which],
            recv_sem=recv_sem.at[which],
            device_id={"region": to},
        ).start()

    def wait_rows(sem, which, count):
        whole = bulk_in.at[pl.ds(0, count)]
        pltpu.make_async_copy(whole, whole, sem.at[which]).wait()

    pl.semaphore_wait(barrier, regions - 1 + lanes - 1)

    def send_small(j, carry):
        send_row(small_out, small_in, 0, j, ahead(j))
        return carry

    lax.fori_loop(1, regions, send_small, 0)
    chunk = MSG // CHUNKS
    for h in range(CHUNKS):

        def send_chunk(j, carry, h=h):
            at = pl.ds(pl.multiple_of((j - 1) * MSG + h * chunk, 8), chunk)
            pltpu.make_async_remote_copy(
                src_ref=bulk_out.at[at],
                dst_ref=bulk_in.at[at],
                send_sem=send_sem.at[1 + h],
                recv_sem=recv_sem.at[1 + h],
                device_id={"region": ahead(j)},
            ).start()
            return carry

        def send_both(j, carry, send_chunk=send_chunk):
            return send_chunk(regions - j, send_chunk(j, carry))

        lax.fori_loop(1, regions // 2, send_both, 0)
        send_chunk(regions // 2, 0)

    for m in range(3):
        xs[m, 0:pairs, :] = points[m].astype(F32)
    cw[0:pairs, :] = conf[0].astype(F32) * weight_column[0:pairs]
    def one_hots(column, count):
        key_ids = lax.broadcasted_iota(jnp.int32, (count, gather_hot.shape[1]), 1)
        for n in (2, 1):
            key_ids = jnp.where(key_ids >= n * keys, jnp.where(key_ids < 3 * keys, key_ids - n * keys, -1), key_ids)
        return jnp.where(column == key_ids.astype(F32), 1.0, 0.0)

    hot = one_hots(jnp.concatenate([as_column(firsts)[0:near_at], near], 0), pair_lanes)
    gather_hot[0:pair_lanes, :] = hot.astype(BF16)
    scatter_hot[:, 0:pair_lanes] = jnp.transpose(hot[:, 0:128]).astype(BF16)
    place_ids = lax.broadcasted_iota(jnp.int32, back_hot.shape, 1).astype(F32)
    back_hot[...] = jnp.where(as_column(place) == place_ids, 1.0, 0.0).astype(BF16)

    column_ids = lax.broadcasted_iota(jnp.int32, (8, 128), 1)
    down_step = 8.0 * (128 // ANCH_W)
    row_ids = lax.broadcasted_iota(jnp.int32, (128, 128), 0)
    anchor = lax.broadcasted_iota(jnp.int32, (128, 128), 1)
    anchor_row = lax.div(anchor, jnp.full_like(anchor, ANCH_W))
    across = (8 * (anchor - anchor_row * ANCH_W) + 4 - 4 * ANCH_W).astype(F32)
    downward = (8 * anchor_row + 4 - 4 * ANCH_H).astype(F32)
    kind = lax.rem(row_ids, jnp.full_like(row_ids, COEFS))
    kind = jnp.where(row_ids < 3 * COEFS, kind, -1)
    for k in range(3):
        ray = jnp.where(kind == 4 * k, across, jnp.where(kind == 4 * k + 1, downward, jnp.where(kind == 4 * k + 2, 1.0, 0.0)))
        step = jnp.where(kind == 4 * k + 1, down_step, 0.0)
        move = jnp.where(kind == 4 * k + 3, 1.0, 0.0)
        for b, value in ((k, ray), (3 + k, step), (6 + k, move)):
            camera_ones[:, 128 * b : 128 * b + 128] = value.astype(BF16)
        for j in range(4):
            b = 4 * k + j
            pose_ones[:, 128 * b : 128 * b + 128] = jnp.where(kind == b, 1.0, 0.0).astype(BF16)
    across = across[0:8, :]
    downward = downward[0:8, :]

    for padded, values in ((cam, cam_in), (cmean, cmean_in), (csq, csq_in)):
        padded[...] = jnp.ones((8, 128), F32)
        padded[:, 0:own] = values[...]
    narrow[...] = jnp.zeros_like(narrow)
    rows_g[...] = jnp.zeros_like(rows_g)
    rows_s[...] = jnp.zeros_like(rows_s)
    table[...] = jnp.zeros_like(table)
    small_table[...] = jnp.zeros_like(small_table)

    def small_copy(it, phase, src, dst, device_id):
        return pltpu.make_async_remote_copy(
            src_ref=src,
            dst_ref=dst,
            send_sem=small_send.at[16 * it + phase],
            recv_sem=small_recv.at[16 * it + phase],
            device_id=device_id,
        )

    def fill_table(at, depth, coefs):
        for n, piece in enumerate(split_three(depth)):
            table[n * keys + at : n * keys + at + depth.shape[0], :] = piece
        for n, piece in enumerate(split_three(coefs)):
            small_table[n * keys + at : n * keys + at + depth.shape[0], :] = piece

    def gather(at, count):
        hot = gather_hot[at : at + count, :]
        for n in range(0, ANCH, 256):
            rows_d[at : at + count, n : n + 256] = dot(hot, table[:, n : n + 256])
        rows_c[at : at + count, :] = dot(pack_three(dot(hot, small_table[...])), camera_ones[...])

    def pose_rows(at, values):
        rows_p[at : at + values.shape[0], :] = dot(pack_three(values), pose_ones[...])

    def group(g, inner):
        at = pl.ds(pl.multiple_of(g * 8, 8), 8)

        def block(ref, b):
            return ref[at, 128 * b : 128 * b + 128]

        shift = [[block(rows_p, 4 * k + j) for j in range(4)] for k in range(3)]
        ray = [block(rows_c, k) for k in range(3)]
        zero = jnp.zeros((8, 128), F32)
        turned = [[zero for j in range(3)] for k in range(3)]
        total = [zero for k in range(3)]
        by_depth = [zero for k in range(3)]
        by_down = [zero for k in range(3)]
        for t in range(TILES):
            part = slice(128 * t, 128 * t + 128)
            d = rows_d[at, part]
            c = cw[at, part]
            x = [xs[j, at, part] for j in range(3)]
            along = None
            for k in range(3):
                placed = shift[k][0] * x[0] + shift[k][1] * x[1] + (shift[k][2] * x[2] + shift[k][3])
                pull = c * ((d * ray[k] + block(rows_c, 6 + k)) - placed)
                for j in range(3):
                    turned[k][j] = turned[k][j] + pull * x[j]
                total[k] = total[k] + pull
                deep = pull * d
                by_depth[k] = by_depth[k] + deep
                if t > 0:
                    by_down[k] = by_down[k] + F32(t) * deep
                along = deep * ray[k] if along is None else along + deep * ray[k]
                if t < TILES - 1:
                    ray[k] = ray[k] + block(rows_c, 3 + k)
            rows_g[at, part] = along
        out = zero
        for k in range(3):
            values = [by_depth[k] * across, by_depth[k] * downward + by_down[k] * down_step, by_depth[k], total[k]]
            for j in range(4):
                out = jnp.where(column_ids == 4 * k + j, jnp.sum(values[j], axis=1, keepdims=True), out)
            for j in range(3):
                column = COEFS + 4 * k + j
                out = jnp.where(column_ids == column, jnp.sum(turned[k][j], axis=1, keepdims=True), out)
        rows_s[at, :] = out
        return inner

    def iteration(it, carry):
        first = it == 0
        q = [cam[k : k + 1, :] for k in range(4)]
        turn, turn_inverse = rotation_rows(*q)
        near_focal = jnp.exp(-cam[7:8, :])
        for k in range(3):
            narrow[4 * k : 4 * k + 1, :] = turn[k][0] * near_focal
            narrow[4 * k + 1 : 4 * k + 2, :] = turn[k][1] * near_focal
            narrow[4 * k + 2 : 4 * k + 3, :] = turn[k][2]
            narrow[4 * k + 3 : 4 * k + 4, :] = cam[4 + k : 5 + k, :]
        coefs = jnp.transpose(narrow[...])[0:own, :]
        depth = jnp.exp(logd[it])
        edge_d[it, 0] = depth[0:EDGE, :]
        edge_c[it, 0] = coefs[0:EDGE, :]
        edge_copies = [
            small_copy(it, 0, edge_d.at[it, 0], edge_d.at[it, 1], {"region": behind(1)}),
            small_copy(it, 1, edge_c.at[it, 0], edge_c.at[it, 1], {"region": behind(1)}),
        ]
        for copy in edge_copies:
            copy.start()
        fill_table(0, depth, coefs)
        gather(0, near_at)

        def pair_coefs():
            p = [pose[k : k + 1, :] for k in range(4)]
            bend, bend_inverse = rotation_rows(*p)
            scale = jnp.exp(pose[7:8, :])
            for k in range(3):
                for j in range(3):
                    wide[4 * k + j : 4 * k + j + 1, :] = scale * bend[k][j]
                wide[4 * k + 3 : 4 * k + 4, :] = scale * pose[4 + k : 5 + k, :]
            return jnp.transpose(wide[...])

        @pl.when(first)
        def _():
            values = pair_coefs()
            near_values = dot_exact(pick_hot[slots : slots + nearby, :], values[0:pair_lanes])
            pose_rows(0, jnp.concatenate([values[0:near_at], near_values], 0))

        lax.fori_loop(0, near_at // 8, group, 0)

        @pl.when(first)
        def _():
            found = dot_exact(pick_hot[0:slots, :], rows_s[0:pair_lanes, :])
            first_out[...] = halves(found)

            def send(j, inner):
                send_row(first_out, first_in, 1 + CHUNKS, j, ahead(j))
                return inner

            lax.fori_loop(1, regions, send, 0)

        for copy in edge_copies:
            copy.wait_recv()
        fill_table(
            own,
            jnp.concatenate([edge_d[it, 1], jnp.zeros((8, ANCH), F32)], 0),
            jnp.concatenate([edge_c[it, 1], jnp.zeros((8, 128), F32)], 0),
        )
        gather(near_at, nearby)
        lax.fori_loop(near_at // 8, pair_lanes // 8, group, 0)
        hot = scatter_hot[0:keys, 0:pair_lanes]
        for n in range(0, ANCH, 256):
            high, low = split_two(rows_g[0:pair_lanes, n : n + 256])
            grad_d[:, n : n + 256] = dot(hot, high) + dot(hot, low)
        grad_s[...] = dot_exact(hot, rows_s[0:pair_lanes, :])
        back_d[it, 0] = grad_d[own : own + EDGE, :]
        back_c[it, 0] = grad_s[own : own + EDGE, :]
        back_copies = [
            small_copy(it, 2, back_d.at[it, 0], back_d.at[it, 1], {"region": ahead(1)}),
            small_copy(it, 3, back_c.at[it, 0], back_c.at[it, 1], {"region": ahead(1)}),
        ]
        for copy in back_copies:
            copy.start()

        @pl.when(first)
        def _():
            wait_rows(recv_sem, 0, regions - 1)
            named = from_halves(small_in[...])
            hot = one_hots(named[:, 24:25], slots)
            gather_hot[pair_lanes : pair_lanes + slots, :] = hot.astype(BF16)
            if slots < 128:
                hot = jnp.concatenate([hot, jnp.zeros((128 - slots, hot.shape[1]), F32)], 0)
                named = jnp.concatenate([named, jnp.ones((128 - slots, 128), F32)], 0)
            scatter_hot[:, pair_lanes:total_rows] = jnp.transpose(hot[:, 0:128]).astype(BF16)
            named = jnp.transpose(named)
            pose[:, pair_lanes:total_rows] = named[0:8, :]
            pmean[:, pair_lanes:total_rows] = named[8:16, :]
            psq[:, pair_lanes:total_rows] = named[16:24, :]
            values = pair_coefs()
            pose_rows(pair_lanes, values[pair_lanes : pair_lanes + slots])
            for h in range(CHUNKS):
                wait_rows(recv_sem, 1 + h, chunk * (regions - 1))
            bulk_in[MSG * (regions - 1) : MSG * regions, :] = jnp.zeros((MSG, 128), F32)
            for c in range(CAP):
                for g in range(regions // 8):
                    at = pair_lanes + c * regions + 8 * g
                    for t in range(TILES):
                        for m in range(MAPS):
                            source = MSG * 8 * g + CAP * MAPS * t + MAPS * c + m
                            value = bulk_in[pl.ds(source, 8, stride=MSG), :]
                            if m < 3:
                                xs[m, at : at + 8, 128 * t : 128 * t + 128] = value
                            else:
                                cw[at : at + 8, 128 * t : 128 * t + 128] = value

        gather(pair_lanes, slots)
        lax.fori_loop(pair_lanes // 8, (pair_lanes + slots) // 8, group, 0)
        second_out[it] = halves(rows_s[pair_lanes : pair_lanes + slots, :])

        def send_back(j, inner):
            send_row(second_out.at[it], second_in.at[it], 2 + CHUNKS + it, j, behind(j))
            return inner

        lax.fori_loop(1, regions, send_back, 0)
        hot = scatter_hot[0:own, pair_lanes:total_rows]
        for n in range(0, ANCH, 256):
            high, low = split_two(rows_g[pair_lanes:total_rows, n : n + 256])
            grad_d[0:own, n : n + 256] = grad_d[0:own, n : n + 256] + (dot(hot, high) + dot(hot, low))
        sums = grad_s[0:own, :] + dot_exact(hot, rows_s[pair_lanes:total_rows, :])
        for copy in back_copies:
            copy.wait_recv()
        grad_d[0:EDGE, :] = grad_d[0:EDGE, :] + back_d[it, 1]
        sums = jnp.concatenate([sums[0:EDGE, :] + back_c[it, 1], sums[EDGE:own, :]], 0)
        if own < 128:
            sums = jnp.concatenate([sums, jnp.zeros((128 - own, 128), F32)], 0)
        part_c[it, lane] = jnp.transpose(sums)[0:16, :]

        lane_copies = []
        for k in range(1, lanes):
            to = lane_at(k)
            rows = pl.ds(pl.multiple_of(to * share, share), share)
            lane_copies.append(small_copy(it, 4 + k, grad_d.at[rows], part_d.at[it, k - 1], {"pair": to}))
            lane_copies.append(small_copy(it, 7 + k, part_c.at[it, lane], part_c.at[it, lane], {"pair": to}))
        for copy in lane_copies:
            copy.start()
        for copy in lane_copies:
            copy.wait_recv()
        gradient = grad_d[pl.ds(my_rows, share), :]
        for k in range(1, lanes):
            gradient = gradient + part_d[it, k - 1]
        updated, dmean[...], dsq[...] = adam(logd[it, pl.ds(my_rows, share), :], gradient, dmean[...], dsq[...], first)
        logd[it + 1, pl.ds(my_rows, share), :] = updated
        mine = logd.at[it + 1, pl.ds(my_rows, share)]
        gathers = [small_copy(it, 10 + k, mine, mine, {"pair": lane_at(k)}) for k in range(1, lanes)]
        for copy in gathers:
            copy.start()

        found = part_c[it, 0]
        for k in range(1, lanes):
            found = found + part_c[it, k]
        across_sum = [found[4 * k : 4 * k + 1, :] * near_focal for k in range(3)]
        down_sum = [found[4 * k + 1 : 4 * k + 2, :] * near_focal for k in range(3)]
        g_turn = [[across_sum[k], down_sum[k], found[4 * k + 2 : 4 * k + 3, :]] for k in range(3)]
        g_cam = rotation_pull(q, turn, turn_inverse, g_turn)
        for k in range(3):
            g_cam.append(found[4 * k + 3 : 4 * k + 4, :])
        g_cam.append(-sum(turn[k][0] * across_sum[k] + turn[k][1] * down_sum[k] for k in range(3)))
        for k in range(8):
            row = slice(k, k + 1)
            cam[row, :], cmean[row, :], csq[row, :] = adam(cam[row, :], g_cam[k], cmean[row, :], csq[row, :], first)

        @pl.when(first)
        def _():
            wait_rows(recv_sem, 1 + CHUNKS, regions - 1)
            first_in[regions - 1 : regions, :] = jnp.zeros((1, 128), F32)

        wait_rows(recv_sem, 2 + CHUNKS + it, regions - 1)
        second_in[it, regions - 1 : regions, :] = jnp.zeros((1, 128), F32)
        seconds = jnp.concatenate([from_halves(second_in[it]), rows_s[near_at:pair_lanes, :]], 0)
        of_pairs = dot_exact(back_hot[...], seconds)
        of_pairs = jnp.concatenate([of_pairs[0:near_at] + rows_s[0:near_at, :], of_pairs[near_at:pair_lanes]], 0)
        of_slots = from_halves(first_in[...]) + rows_s[pair_lanes : pair_lanes + slots, :]
        if slots < total_rows - pair_lanes:
            of_slots = jnp.concatenate([of_slots, jnp.zeros((total_rows - pair_lanes - slots, 128), F32)], 0)
        found = jnp.transpose(jnp.concatenate([of_pairs, of_slots], 0))
        m = [[found[COEFS + 4 * k + j : COEFS + 4 * k + j + 1, :] for j in range(3)] for k in range(3)]
        v = [found[4 * k + 3 : 4 * k + 4, :] for k in range(3)]
        p = [pose[k : k + 1, :] for k in range(4)]
        bend, bend_inverse = rotation_rows(*p)
        scale = jnp.exp(pose[7:8, :])
        g_turn = [[-(scale * m[k][j]) for j in range(3)] for k in range(3)]
        g_pose = rotation_pull(p, bend, bend_inverse, g_turn)
        g_scale = sum(bend[k][j] * g_turn[k][j] for k in range(3) for j in range(3))
        for k in range(3):
            g_move = -(scale * v[k])
            g_scale = g_scale + pose[4 + k : 5 + k, :] * g_move
            g_pose.append(g_move)
        g_pose.append(g_scale)
        for k in range(8):
            row = slice(k, k + 1)
            pose[row, :], pmean[row, :], psq[row, :] = adam(pose[row, :], g_pose[k], pmean[row, :], psq[row, :], first)

        @pl.when(it < ITERS - 1)
        def _():
            values = pair_coefs()
            near_values = dot_exact(pick_hot[slots : slots + nearby, :], values[0:pair_lanes])
            pose_rows(0, jnp.concatenate([values[0:near_at], near_values, values[pair_lanes : pair_lanes + slots]], 0))

        for copy in lane_copies + edge_copies + back_copies:
            copy.wait_send()
        for copy in gathers:
            copy.wait()
        return carry

    lax.fori_loop(0, ITERS, iteration, 0)

    wait_rows(send_sem, 0, regions - 1)
    for h in range(CHUNKS):
        wait_rows(send_sem, 1 + h, chunk * (regions - 1))
    for n in range(1 + ITERS):
        wait_rows(send_sem, 1 + CHUNKS + n, regions - 1)
    cam_in[...] = cam[:, 0:own]
    pose_in[...] = pose[:, 0:pairs]
    pmean_in[...] = pmean[:, 0:pairs]
    psq_in[...] = psq[:, 0:pairs]
    for n, src in enumerate((cmean, csq)):
        value = src[:, 0:share]
        for k in range(1, lanes):
            value = jnp.where(lane == k, src[:, k * share : (k + 1) * share], value)
        moments[n] = value
    stores = [
        pltpu.make_async_copy(src, dst, load_sem.at[n])
        for n, (src, dst) in enumerate(
            (
                (logd.at[ITERS], logd_out), (cam_in, cam_out), (pose_in, pose_out), (dmean, dmean_out), (dsq, dsq_out),
                (moments.at[0], cmean_out), (moments.at[1], csq_out), (pmean_in, pmean_out), (psq_in, psq_out),
            )
        )
    ]
    for store in stores:
        store.start()
    for store in stores:
        store.wait()


def deliver(*refs):
    count = (len(refs) - 1) // 2
    copies = [pltpu.make_async_copy(refs[n], refs[count + n], refs[-1].at[n]) for n in range(count)]
    for copy in copies:
        copy.start()
    for copy in copies:
        copy.wait()


def shards(
    log_depth, cameras, pair_pose, depth_mean, depth_square, camera_mean, camera_square, pose_mean, pose_square,
    pointmaps, confidence, pair_images, pair_flag,
):
    regions = lax.axis_size("region")
    lanes = lax.axis_size("pair")
    own = log_depth.shape[0]
    pairs = pair_pose.shape[0]
    share = own // lanes
    slots = CAP * regions
    nearby = pairs - CAP * (regions - 1)
    pair_lanes = rounded(pairs, 128)
    total_rows = pair_lanes + rounded(slots, 128)
    keys = own + 16
    key_lanes = rounded(3 * keys, 128)
    in_hbm = pl.BlockSpec(memory_space=pltpu.HBM)

    def vmem(*shape, dtype=F32):
        return pltpu.VMEM(shape, dtype)

    def out(*shape):
        return jax.ShapeDtypeStruct(shape, F32)

    shapes = (
        out(own, ANCH), out(8, own), out(8, pairs), out(share, ANCH), out(share, ANCH),
        out(8, share), out(8, share), out(8, pairs), out(8, pairs),
    )
    results = pl.pallas_call(
        functools.partial(kernel, regions, lanes, own, pairs),
        out_shape=shapes,
        in_specs=[in_hbm] * 13,
        out_specs=(in_hbm,) * 9,
        scratch_shapes=[
            vmem(8, own), vmem(8, own), vmem(8, own), vmem(8, pairs), vmem(8, pairs), vmem(8, pairs),
            vmem(2, pairs, dtype=jnp.int32), vmem(1, pairs, dtype=jnp.int32),
            vmem(ITERS + 1, own, ANCH), vmem(share, ANCH), vmem(share, ANCH),
            vmem(8, 128), vmem(8, 128), vmem(8, 128),
            vmem(8, total_rows), vmem(8, total_rows), vmem(8, total_rows),
            vmem(6, pairs, ANCH, dtype=BF16), vmem(2, pairs, ANCH, dtype=BF16),
            vmem(3, total_rows, ANCH), vmem(total_rows, ANCH),
            vmem(8, pair_lanes, dtype=jnp.int32),
            vmem(slots + nearby, pair_lanes, dtype=BF16), vmem(pair_lanes, slots + nearby, dtype=BF16),
            vmem(total_rows, key_lanes, dtype=BF16), vmem(128, total_rows, dtype=BF16),
            vmem(128, 9 * 128, dtype=BF16), vmem(128, 12 * 128, dtype=BF16),
            vmem(key_lanes, ANCH, dtype=BF16), vmem(key_lanes, 128, dtype=BF16),
            vmem(total_rows, ANCH), vmem(total_rows, 9 * 128), vmem(total_rows, 12 * 128),
            vmem(total_rows, ANCH), vmem(total_rows, 128),
            vmem(128, total_rows), vmem(128, 128), vmem(keys, ANCH), vmem(keys, 128),
            vmem(regions, 128), vmem(regions, 128), vmem(MSG * regions, 128), vmem(MSG * regions, 128),
            vmem(regions, 128), vmem(regions, 128), vmem(ITERS, regions, 128), vmem(ITERS, regions, 128),
            vmem(ITERS, 2, EDGE, ANCH), vmem(ITERS, 2, EDGE, 128),
            vmem(ITERS, 2, EDGE, ANCH), vmem(ITERS, 2, EDGE, 128),
            vmem(ITERS, lanes - 1, share, ANCH), vmem(ITERS, lanes, 16, 128), vmem(2, 8, share),
            pltpu.SemaphoreType.DMA((13,)),
            pltpu.SemaphoreType.DMA((2 + CHUNKS + ITERS,)), pltpu.SemaphoreType.DMA((2 + CHUNKS + ITERS,)),
            pltpu.SemaphoreType.DMA((16 * ITERS,)), pltpu.SemaphoreType.DMA((16 * ITERS,)),
        ],
        compiler_params=pltpu.CompilerParams(
            collective_id=0, has_side_effects=True, vmem_limit_bytes=62 * 1024 * 1024
        ),
        name="align",
    )(
        log_depth, cameras.T, pair_pose.T, depth_mean, depth_square, camera_mean.T, camera_square.T,
        pose_mean.T, pose_square.T, pointmaps.transpose(1, 0, 2), confidence.transpose(1, 0, 2),
        pair_images.T, pair_flag.reshape(1, pairs),
    )
    depth, camera, pose, dmean, dsq, cmean, csq, pmean, psq = pl.pallas_call(
        deliver,
        out_shape=shapes,
        in_specs=[in_hbm] * 9,
        out_specs=(in_hbm,) * 9,
        scratch_shapes=[pltpu.SemaphoreType.DMA((9,))],
        compiler_params=pltpu.CompilerParams(vmem_limit_bytes=62 * 1024 * 1024),
        name="deliver",
    )(*results)
    return depth, camera.T, pose.T, dmean, dsq, cmean.T, csq.T, pmean.T, psq.T


def solution(mesh):
    placed = (
        P("region", None),
        P("region", None),
        P(("region", "pair"), None),
        P("region", None),
        P("region", None),
        P("region", None),
        P("region", None),
        P(("region", "pair"), None),
        P(("region", "pair"), None),
        P(("region", "pair"), None, None),
        P(("region", "pair"), None, None),
        P(("region", "pair"), None),
        P(("region", "pair")),
    )
    return jax.shard_map(
        shards,
        mesh=mesh,
        in_specs=placed,
        out_specs=(
            P("region", None),
            P("region", None),
            P(("region", "pair"), None),
            P(("region", "pair"), None),
            P(("region", "pair"), None),
            P(("region", "pair"), None),
            P(("region", "pair"), None),
            P(("region", "pair"), None),
            P(("region", "pair"), None),
        ),
        check_vma=False,
    )
```

time: 136 us -> 99.6 us (0.73)
  Pallas kernels: 118 us -> 96.9 us
  local copies, waits for them, and re-layouts: 16.4 us -> 1.93 us
    pallas_call x1, Pallas kernels: 118 us -> 85.6 us  [shards(): pl.pallas_call(functools.partial(kernel, regions, lanes, own, pairs), out...]
    unnamed x34 -> x1, local copies, waits for them, and re-layouts: 16.4 us -> 1.93 us
    pallas_call x0 -> x1, Pallas kernels: none -> 11.2 us  [shards(): pl.pallas_call(deliver, out_shape=shapes, in_specs=[in_hbm] * 9, out_spec...]
where the time goes in v2:
time: 99.6 us; the launch traced here: 99.5 us
  Pallas kernels  96.9 us (97%)
  local copies, waits for them, and re-layouts  1.93 us (2%)
    pallas_call x1, Pallas kernels, shards(): pl.pallas_call(functools.partial(kernel, regions, lanes, own, pairs), out...  85.6 us
    pallas_call x1, Pallas kernels, shards(): pl.pallas_call(deliver, out_shape=shapes, in_specs=[in_hbm] * 9, out_spec...  11.2 us

profile of v2, /device:TPU:4, one launch (start us, length us, event | category | flops | bytes accessed | tf_op | source)
XLA Modules:
  0.0 99.5 jit_solution(6213693408197241287)
XLA Ops:
  0.6 1.9 %copy.24 = bf16[190,2,768]{2,0,1:T(8,128)(2,1)} copy(bf16[190,2,768]{2,1,0:T(2,128)(2,1)} %param.23) | data formatting | bytes 1167360 | tf_op args[10]
  2.6 85.6 %align.1 = (f32[64,768]{1,0:T(8,128)}, f32[8,64]{1,0:T(8,128)}, f32[8,190]{1,0:T(8,128)}, f32[16,768]{1,0:T(8,128)}, f32[16,768]{1,0:T(8,128)}, /*index=5*/f32[8...) custom-call(f32[64,768]{1,0:T(8,128)} %logd_hbm.1, f32[8,64]{1,0:T(8,128)} %bitcast.23, ...), custom_call_target="tpu_custom_call" | custom-call | tf_op jit(solution)/shard_map/align/pallas_call | solution.py:670
  88.2 11.2 %deliver.1 = (f32[64,768]{1,0:T(8,128)}, f32[8,64]{1,0:T(8,128)}, f32[8,190]{1,0:T(8,128)}, f32[16,768]{1,0:T(8,128)}, f32[16,768]{1,0:T(8,128)}, /*index=5*/f32...) custom-call(f32[64,768]{1,0:T(8,128)} %get-tuple-element.27.refs_0_, ...), custom_call_target="tpu_custom_call" | custom-call | tf_op jit(solution)/shard_map/deliver/pallas_call | solution.py:709

commit v3 on v2

--- a/solution.py
+++ b/solution.py
@@ -98,10 +98,9 @@
     return [twice * (g_w - w * along), twice * (g_x - x * along), twice * (g_y - y * along), twice * (g_z - z * along)]
 
 
-def adam(param, gradient, mean, square, first):
-    fixes = [(1.0 - BETA_ONE ** (START + 1 + i), 1.0 - BETA_TWO ** (START + 1 + i)) for i in range(ITERS)]
-    fix_one = jnp.where(first, F32(fixes[0][0]), F32(fixes[1][0]))
-    fix_two = jnp.where(first, F32(fixes[0][1]), F32(fixes[1][1]))
+def adam(param, gradient, mean, square, it):
+    fix_one = 1.0 - BETA_ONE ** (START + 1 + it)
+    fix_two = 1.0 - BETA_TWO ** (START + 1 + it)
     mean = BETA_ONE * mean + (1.0 - BETA_ONE) * gradient
     square = BETA_TWO * square + (1.0 - BETA_TWO) * gradient * gradient
     param = param - LEARN_RATE * (mean / fix_one) / (jnp.sqrt(square / fix_two) + EPSILON)
@@ -118,7 +117,7 @@
     index_rows, pick_hot, back_hot, gather_hot, scatter_hot, camera_ones, pose_ones,
     table, small_table, rows_d, rows_c, rows_p, rows_g, rows_s, wide, narrow, grad_d, grad_s,
     small_out, small_in, bulk_out, bulk_in, first_out, first_in, second_out, second_in,
-    edge_d, edge_c, back_d, back_c, part_d, part_c, moments,
+    edge_d, edge_c, back_d, back_c, part_d, part_e, part_c, moments,
     load_sem, send_sem, recv_sem, small_send, small_recv,
 ):
     share = own // lanes
@@ -164,6 +163,12 @@
     lax.fori_loop(1, regions, greet, 0)
     for k in range(1, lanes):
         pl.semaphore_signal(barrier, inc=1, device_id={"pair": lane_at(k)})
+
+
+    @pl.when(lane == 0)
+    def _():
+        for k in range(1, lanes):
+            pl.semaphore_signal(barrier, inc=1, device_id={"region": behind(1), "pair": k})
 
     for load in loads:
         load.wait()
@@ -219,6 +224,10 @@
 
     small_out[...] = halves(details)
     small_in[regions - 1 : regions, :] = jnp.ones((1, 128), F32)
+    bulk_in[MSG * (regions - 1) : MSG * regions, :] = jnp.zeros((MSG, 128), F32)
+    first_in[regions - 1 : regions, :] = jnp.zeros((1, 128), F32)
+    for it in range(ITERS):
+        second_in[it, regions - 1 : regions, :] = jnp.zeros((1, 128), F32)
     weights = 2.0 * (1.0 + flags.astype(F32))
     weights = jnp.where(real, weights, 0.0)
     weight_column = as_column(weights)
@@ -255,7 +264,7 @@
         whole = bulk_in.at[pl.ds(0, count)]
         pltpu.make_async_copy(whole, whole, sem.at[which]).wait()
 
-    pl.semaphore_wait(barrier, regions - 1 + lanes - 1)
+    pl.semaphore_wait(barrier, regions - 1 + lanes - 1 + jnp.where(lane == 0, 0, 1))
 
     def send_small(j, carry):
         send_row(small_out, small_in, 0, j, ahead(j))
@@ -327,31 +336,34 @@
     table[...] = jnp.zeros_like(table)
     small_table[...] = jnp.zeros_like(small_table)
 
-    def small_copy(it, phase, src, dst, device_id):
+    counter = iter(range(small_send.shape[0]))
+
+    def small_copy(src, dst, device_id):
+        which = next(counter)
         return pltpu.make_async_remote_copy(
             src_ref=src,
             dst_ref=dst,
-            send_sem=small_send.at[16 * it + phase],
-            recv_sem=small_recv.at[16 * it + phase],
+            send_sem=small_send.at[which],
+            recv_sem=small_recv.at[which],
             device_id=device_id,
         )
 
-    def fill_table(at, depth, coefs):
-        for n, piece in enumerate(split_three(depth)):
-            table[n * keys + at : n * keys + at + depth.shape[0], :] = piece
-        for n, piece in enumerate(split_three(coefs)):
-            small_table[n * keys + at : n * keys + at + depth.shape[0], :] = piece
-
-    def gather(at, count):
-        hot = gather_hot[at : at + count, :]
-        for n in range(0, ANCH, 256):
-            rows_d[at : at + count, n : n + 256] = dot(hot, table[:, n : n + 256])
-        rows_c[at : at + count, :] = dot(pack_three(dot(hot, small_table[...])), camera_ones[...])
+    def fill(ref, at, values):
+        for n, piece in enumerate(split_three(values)):
+            ref[n * keys + at : n * keys + at + values.shape[0], 0 : values.shape[1]] = piece
+
+    def gather_depths(at, count, begin=0, end=ANCH):
+        for n in range(begin, end, 256):
+            rows_d[at : at + count, n : n + 256] = dot(gather_hot[at : at + count, :], table[:, n : n + 256])
+
+    def gather_cameras(at, count):
+        values = dot(gather_hot[at : at + count, :], small_table[...])
+        rows_c[at : at + count, :] = dot(pack_three(values), camera_ones[...])
 
     def pose_rows(at, values):
         rows_p[at : at + values.shape[0], :] = dot(pack_three(values), pose_ones[...])
 
-    def group(g, inner):
+    def group(g, inner, begin=0, end=TILES):
         at = pl.ds(pl.multiple_of(g * 8, 8), 8)
 
         def block(ref, b):
@@ -359,12 +371,14 @@
 
         shift = [[block(rows_p, 4 * k + j) for j in range(4)] for k in range(3)]
         ray = [block(rows_c, k) for k in range(3)]
+        if begin > 0:
+            ray = [ray[k] + F32(begin) * block(rows_c, 3 + k) for k in range(3)]
         zero = jnp.zeros((8, 128), F32)
         turned = [[zero for j in range(3)] for k in range(3)]
         total = [zero for k in range(3)]
         by_depth = [zero for k in range(3)]
         by_down = [zero for k in range(3)]
-        for t in range(TILES):
+        for t in range(begin, end):
             part = slice(128 * t, 128 * t + 128)
             d = rows_d[at, part]
             c = cw[at, part]
@@ -381,7 +395,7 @@
                 if t > 0:
                     by_down[k] = by_down[k] + F32(t) * deep
                 along = deep * ray[k] if along is None else along + deep * ray[k]
-                if t < TILES - 1:
+                if t < end - 1:
                     ray[k] = ray[k] + block(rows_c, 3 + k)
             rows_g[at, part] = along
         out = zero
@@ -392,157 +406,140 @@
             for j in range(3):
                 column = COEFS + 4 * k + j
                 out = jnp.where(column_ids == column, jnp.sum(turned[k][j], axis=1, keepdims=True), out)
-        rows_s[at, :] = out
+        rows_s[at, :] = out if begin == 0 else rows_s[at, :] + out
         return inner
 
-    def iteration(it, carry):
-        first = it == 0
+    def groups(at, count, begin=0, end=TILES):
+        lax.fori_loop(at // 8, (at + count) // 8, functools.partial(group, begin=begin, end=end), 0)
+
+    def scatter(rows, keys_from, keys_to, begin=0, end=ANCH):
+        hot = scatter_hot[keys_from:keys_to, rows]
+        for n in range(begin, end, 256):
+            high, low = split_two(rows_g[rows, n : n + 256])
+            yield slice(n, n + 256), dot(hot, high) + dot(hot, low)
+
+    def camera_parts():
         q = [cam[k : k + 1, :] for k in range(4)]
         turn, turn_inverse = rotation_rows(*q)
-        near_focal = jnp.exp(-cam[7:8, :])
+        return q, turn, turn_inverse, jnp.exp(-cam[7:8, :])
+
+    def camera_coefs(it):
+        q, turn, turn_inverse, near_focal = camera_parts()
         for k in range(3):
             narrow[4 * k : 4 * k + 1, :] = turn[k][0] * near_focal
             narrow[4 * k + 1 : 4 * k + 2, :] = turn[k][1] * near_focal
             narrow[4 * k + 2 : 4 * k + 3, :] = turn[k][2]
             narrow[4 * k + 3 : 4 * k + 4, :] = cam[4 + k : 5 + k, :]
         coefs = jnp.transpose(narrow[...])[0:own, :]
+        edge_c[it, 0] = coefs[0:EDGE, :]
+        copy = small_copy(edge_c.at[it, 0], edge_c.at[it, 1], {"region": behind(1)})
+        copy.start()
+        fill(small_table, 0, coefs)
+        return copy
+
+    def pair_coefs():
+        p = [pose[k : k + 1, :] for k in range(4)]
+        bend, bend_inverse = rotation_rows(*p)
+        scale = jnp.exp(pose[7:8, :])
+        for k in range(3):
+            for j in range(3):
+                wide[4 * k + j : 4 * k + j + 1, :] = scale * bend[k][j]
+            wide[4 * k + 3 : 4 * k + 4, :] = scale * pose[4 + k : 5 + k, :]
+        return jnp.transpose(wide[...])
+
+    def pair_rows(with_slots):
+        values = pair_coefs()
+        near_values = dot_exact(pick_hot[slots : slots + nearby, :], values[0:pair_lanes])
+        values = [values[0:near_at], near_values] + ([values[pair_lanes : pair_lanes + slots]] if with_slots else [])
+        pose_rows(0, jnp.concatenate(values, 0))
+
+    def depths(it):
         depth = jnp.exp(logd[it])
         edge_d[it, 0] = depth[0:EDGE, :]
-        edge_c[it, 0] = coefs[0:EDGE, :]
-        edge_copies = [
-            small_copy(it, 0, edge_d.at[it, 0], edge_d.at[it, 1], {"region": behind(1)}),
-            small_copy(it, 1, edge_c.at[it, 0], edge_c.at[it, 1], {"region": behind(1)}),
-        ]
-        for copy in edge_copies:
+        copy = small_copy(edge_d.at[it, 0], edge_d.at[it, 1], {"region": behind(1)})
+        copy.start()
+        fill(table, 0, depth)
+        return copy
+
+    def edge_rows(it, copies):
+        for copy in copies:
+            copy.wait_recv()
+        blank = jnp.zeros((8, ANCH), F32)
+        fill(table, own, jnp.concatenate([edge_d[it, 1], blank], 0))
+        fill(small_table, own, jnp.concatenate([edge_c[it, 1], blank[:, 0:128]], 0))
+        gather_depths(near_at, nearby)
+        gather_cameras(near_at, nearby)
+        groups(near_at, nearby)
+
+    def send_edges_back(it):
+        back_d[it] = grad_d[own : own + EDGE, :]
+        back_c[it, 0] = grad_s[own : own + EDGE, :]
+        which = next(counter)
+        to_owner = pltpu.make_async_remote_copy(
+            src_ref=back_d.at[it],
+            dst_ref=part_e.at[it, lane],
+            send_sem=small_send.at[which],
+            recv_sem=small_recv.at[which],
+            device_id={"region": ahead(1), "pair": 0},
+        )
+        copies = [to_owner, small_copy(back_c.at[it, 0], back_c.at[it, 1], {"region": ahead(1)})]
+        for copy in copies:
             copy.start()
-        fill_table(0, depth, coefs)
-        gather(0, near_at)
-
-        def pair_coefs():
-            p = [pose[k : k + 1, :] for k in range(4)]
-            bend, bend_inverse = rotation_rows(*p)
-            scale = jnp.exp(pose[7:8, :])
-            for k in range(3):
-                for j in range(3):
-                    wide[4 * k + j : 4 * k + j + 1, :] = scale * bend[k][j]
-                wide[4 * k + 3 : 4 * k + 4, :] = scale * pose[4 + k : 5 + k, :]
-            return jnp.transpose(wide[...])
-
-        @pl.when(first)
+        return copies, which
+
+    def take_edges(it, which):
+        @pl.when(lane == 0)
         def _():
-            values = pair_coefs()
-            near_values = dot_exact(pick_hot[slots : slots + nearby, :], values[0:pair_lanes])
-            pose_rows(0, jnp.concatenate([values[0:near_at], near_values], 0))
-
-        lax.fori_loop(0, near_at // 8, group, 0)
-
-        @pl.when(first)
-        def _():
-            found = dot_exact(pick_hot[0:slots, :], rows_s[0:pair_lanes, :])
-            first_out[...] = halves(found)
-
-            def send(j, inner):
-                send_row(first_out, first_in, 1 + CHUNKS, j, ahead(j))
-                return inner
-
-            lax.fori_loop(1, regions, send, 0)
-
-        for copy in edge_copies:
+            whole = part_e.at[it]
+            pltpu.make_async_copy(whole, whole, small_recv.at[which]).wait()
+            total = part_e[it, 0]
+            for k in range(1, lanes):
+                total = total + part_e[it, k]
+            grad_d[0:EDGE, :] = grad_d[0:EDGE, :] + total
+
+    def send_shares(it, begin, end):
+        copies = []
+        for k in range(1, lanes):
+            to = lane_at(k)
+            rows = pl.ds(pl.multiple_of(to * share, share), share)
+            columns = pl.ds(begin, end - begin)
+            copies.append(small_copy(grad_d.at[rows, columns], part_d.at[it, k - 1, :, columns], {"pair": to}))
+        for copy in copies:
+            copy.start()
+        return copies
+
+    def update_depths(it, begin, end, copies):
+        for copy in copies:
             copy.wait_recv()
-        fill_table(
-            own,
-            jnp.concatenate([edge_d[it, 1], jnp.zeros((8, ANCH), F32)], 0),
-            jnp.concatenate([edge_c[it, 1], jnp.zeros((8, 128), F32)], 0),
+        columns = slice(begin, end)
+        gradient = grad_d[pl.ds(my_rows, share), columns]
+        for k in range(1, lanes):
+            gradient = gradient + part_d[it, k - 1, :, columns]
+        updated, dmean[:, columns], dsq[:, columns] = adam(
+            logd[it, pl.ds(my_rows, share), columns], gradient, dmean[:, columns], dsq[:, columns], it
         )
-        gather(near_at, nearby)
-        lax.fori_loop(near_at // 8, pair_lanes // 8, group, 0)
-        hot = scatter_hot[0:keys, 0:pair_lanes]
-        for n in range(0, ANCH, 256):
-            high, low = split_two(rows_g[0:pair_lanes, n : n + 256])
-            grad_d[:, n : n + 256] = dot(hot, high) + dot(hot, low)
-        grad_s[...] = dot_exact(hot, rows_s[0:pair_lanes, :])
-        back_d[it, 0] = grad_d[own : own + EDGE, :]
-        back_c[it, 0] = grad_s[own : own + EDGE, :]
-        back_copies = [
-            small_copy(it, 2, back_d.at[it, 0], back_d.at[it, 1], {"region": ahead(1)}),
-            small_copy(it, 3, back_c.at[it, 0], back_c.at[it, 1], {"region": ahead(1)}),
-        ]
-        for copy in back_copies:
+        logd[it + 1, pl.ds(my_rows, share), columns] = updated
+        mine = logd.at[it + 1, pl.ds(my_rows, share), pl.ds(begin, end - begin)]
+        gathers = [small_copy(mine, mine, {"pair": lane_at(k)}) for k in range(1, lanes)]
+        for copy in gathers:
             copy.start()
-
-        @pl.when(first)
-        def _():
-            wait_rows(recv_sem, 0, regions - 1)
-            named = from_halves(small_in[...])
-            hot = one_hots(named[:, 24:25], slots)
-            gather_hot[pair_lanes : pair_lanes + slots, :] = hot.astype(BF16)
-            if slots < 128:
-                hot = jnp.concatenate([hot, jnp.zeros((128 - slots, hot.shape[1]), F32)], 0)
-                named = jnp.concatenate([named, jnp.ones((128 - slots, 128), F32)], 0)
-            scatter_hot[:, pair_lanes:total_rows] = jnp.transpose(hot[:, 0:128]).astype(BF16)
-            named = jnp.transpose(named)
-            pose[:, pair_lanes:total_rows] = named[0:8, :]
-            pmean[:, pair_lanes:total_rows] = named[8:16, :]
-            psq[:, pair_lanes:total_rows] = named[16:24, :]
-            values = pair_coefs()
-            pose_rows(pair_lanes, values[pair_lanes : pair_lanes + slots])
-            for h in range(CHUNKS):
-                wait_rows(recv_sem, 1 + h, chunk * (regions - 1))
-            bulk_in[MSG * (regions - 1) : MSG * regions, :] = jnp.zeros((MSG, 128), F32)
-            for c in range(CAP):
-                for g in range(regions // 8):
-                    at = pair_lanes + c * regions + 8 * g
-                    for t in range(TILES):
-                        for m in range(MAPS):
-                            source = MSG * 8 * g + CAP * MAPS * t + MAPS * c + m
-                            value = bulk_in[pl.ds(source, 8, stride=MSG), :]
-                            if m < 3:
-                                xs[m, at : at + 8, 128 * t : 128 * t + 128] = value
-                            else:
-                                cw[at : at + 8, 128 * t : 128 * t + 128] = value
-
-        gather(pair_lanes, slots)
-        lax.fori_loop(pair_lanes // 8, (pair_lanes + slots) // 8, group, 0)
-        second_out[it] = halves(rows_s[pair_lanes : pair_lanes + slots, :])
-
-        def send_back(j, inner):
-            send_row(second_out.at[it], second_in.at[it], 2 + CHUNKS + it, j, behind(j))
-            return inner
-
-        lax.fori_loop(1, regions, send_back, 0)
-        hot = scatter_hot[0:own, pair_lanes:total_rows]
-        for n in range(0, ANCH, 256):
-            high, low = split_two(rows_g[pair_lanes:total_rows, n : n + 256])
-            grad_d[0:own, n : n + 256] = grad_d[0:own, n : n + 256] + (dot(hot, high) + dot(hot, low))
-        sums = grad_s[0:own, :] + dot_exact(hot, rows_s[pair_lanes:total_rows, :])
-        for copy in back_copies:
-            copy.wait_recv()
-        grad_d[0:EDGE, :] = grad_d[0:EDGE, :] + back_d[it, 1]
+        return gathers
+
+    def send_cameras(it, sums, back_copy):
+        back_copy.wait_recv()
         sums = jnp.concatenate([sums[0:EDGE, :] + back_c[it, 1], sums[EDGE:own, :]], 0)
         if own < 128:
             sums = jnp.concatenate([sums, jnp.zeros((128 - own, 128), F32)], 0)
         part_c[it, lane] = jnp.transpose(sums)[0:16, :]
-
-        lane_copies = []
-        for k in range(1, lanes):
-            to = lane_at(k)
-            rows = pl.ds(pl.multiple_of(to * share, share), share)
-            lane_copies.append(small_copy(it, 4 + k, grad_d.at[rows], part_d.at[it, k - 1], {"pair": to}))
-            lane_copies.append(small_copy(it, 7 + k, part_c.at[it, lane], part_c.at[it, lane], {"pair": to}))
-        for copy in lane_copies:
+        copies = [small_copy(part_c.at[it, lane], part_c.at[it, lane], {"pair": lane_at(k)}) for k in range(1, lanes)]
+        for copy in copies:
             copy.start()
-        for copy in lane_copies:
+        return copies
+
+    def update_cameras(it, copies):
+        for copy in copies:
             copy.wait_recv()
-        gradient = grad_d[pl.ds(my_rows, share), :]
-        for k in range(1, lanes):
-            gradient = gradient + part_d[it, k - 1]
-        updated, dmean[...], dsq[...] = adam(logd[it, pl.ds(my_rows, share), :], gradient, dmean[...], dsq[...], first)
-        logd[it + 1, pl.ds(my_rows, share), :] = updated
-        mine = logd.at[it + 1, pl.ds(my_rows, share)]
-        gathers = [small_copy(it, 10 + k, mine, mine, {"pair": lane_at(k)}) for k in range(1, lanes)]
-        for copy in gathers:
-            copy.start()
-
+        q, turn, turn_inverse, near_focal = camera_parts()
         found = part_c[it, 0]
         for k in range(1, lanes):
             found = found + part_c[it, k]
@@ -555,58 +552,156 @@
         g_cam.append(-sum(turn[k][0] * across_sum[k] + turn[k][1] * down_sum[k] for k in range(3)))
         for k in range(8):
             row = slice(k, k + 1)
-            cam[row, :], cmean[row, :], csq[row, :] = adam(cam[row, :], g_cam[k], cmean[row, :], csq[row, :], first)
-
-        @pl.when(first)
-        def _():
-            wait_rows(recv_sem, 1 + CHUNKS, regions - 1)
-            first_in[regions - 1 : regions, :] = jnp.zeros((1, 128), F32)
-
+            cam[row, :], cmean[row, :], csq[row, :] = adam(cam[row, :], g_cam[k], cmean[row, :], csq[row, :], it)
+
+    def send_sums(it):
+        second_out[it] = halves(rows_s[pair_lanes : pair_lanes + slots, :])
+
+        def send(j, inner):
+            send_row(second_out.at[it], second_in.at[it], 2 + CHUNKS + it, j, behind(j))
+            return inner
+
+        lax.fori_loop(1, regions, send, 0)
+
+    def update_pairs(it, with_slots):
         wait_rows(recv_sem, 2 + CHUNKS + it, regions - 1)
-        second_in[it, regions - 1 : regions, :] = jnp.zeros((1, 128), F32)
         seconds = jnp.concatenate([from_halves(second_in[it]), rows_s[near_at:pair_lanes, :]], 0)
         of_pairs = dot_exact(back_hot[...], seconds)
-        of_pairs = jnp.concatenate([of_pairs[0:near_at] + rows_s[0:near_at, :], of_pairs[near_at:pair_lanes]], 0)
-        of_slots = from_halves(first_in[...]) + rows_s[pair_lanes : pair_lanes + slots, :]
-        if slots < total_rows - pair_lanes:
-            of_slots = jnp.concatenate([of_slots, jnp.zeros((total_rows - pair_lanes - slots, 128), F32)], 0)
-        found = jnp.transpose(jnp.concatenate([of_pairs, of_slots], 0))
+        found = [of_pairs[0:near_at] + rows_s[0:near_at, :], of_pairs[near_at:pair_lanes]]
+        if with_slots:
+            wait_rows(recv_sem, 1 + CHUNKS, regions - 1)
+            found.append(from_halves(first_in[...]) + rows_s[pair_lanes : pair_lanes + slots, :])
+            if slots < total_rows - pair_lanes:
+                found.append(jnp.zeros((total_rows - pair_lanes - slots, 128), F32))
+        found = jnp.transpose(jnp.concatenate(found, 0))
+        lanes_used = slice(0, total_rows if with_slots else pair_lanes)
         m = [[found[COEFS + 4 * k + j : COEFS + 4 * k + j + 1, :] for j in range(3)] for k in range(3)]
         v = [found[4 * k + 3 : 4 * k + 4, :] for k in range(3)]
-        p = [pose[k : k + 1, :] for k in range(4)]
+        p = [pose[k : k + 1, lanes_used] for k in range(4)]
         bend, bend_inverse = rotation_rows(*p)
-        scale = jnp.exp(pose[7:8, :])
+        scale = jnp.exp(pose[7:8, lanes_used])
         g_turn = [[-(scale * m[k][j]) for j in range(3)] for k in range(3)]
         g_pose = rotation_pull(p, bend, bend_inverse, g_turn)
         g_scale = sum(bend[k][j] * g_turn[k][j] for k in range(3) for j in range(3))
         for k in range(3):
             g_move = -(scale * v[k])
-            g_scale = g_scale + pose[4 + k : 5 + k, :] * g_move
+            g_scale = g_scale + pose[4 + k : 5 + k, lanes_used] * g_move
             g_pose.append(g_move)
         g_pose.append(g_scale)
         for k in range(8):
-            row = slice(k, k + 1)
-            pose[row, :], pmean[row, :], psq[row, :] = adam(pose[row, :], g_pose[k], pmean[row, :], psq[row, :], first)
-
-        @pl.when(it < ITERS - 1)
-        def _():
-            values = pair_coefs()
-            near_values = dot_exact(pick_hot[slots : slots + nearby, :], values[0:pair_lanes])
-            pose_rows(0, jnp.concatenate([values[0:near_at], near_values, values[pair_lanes : pair_lanes + slots]], 0))
-
-        for copy in lane_copies + edge_copies + back_copies:
-            copy.wait_send()
-        for copy in gathers:
-            copy.wait()
-        return carry
-
-    lax.fori_loop(0, ITERS, iteration, 0)
+            row = (slice(k, k + 1), lanes_used)
+            pose[row], pmean[row], psq[row] = adam(pose[row], g_pose[k], pmean[row], psq[row], it)
+
+    near_side = slice(0, pair_lanes)
+    far_side = slice(pair_lanes, total_rows)
+    sent = []
+
+    edges = [camera_coefs(0), depths(0)]
+    sent += edges
+    gather_depths(0, near_at)
+    gather_cameras(0, near_at)
+    pair_rows(False)
+    groups(0, near_at)
+    first_out[...] = halves(dot_exact(pick_hot[0:slots, :], rows_s[0:pair_lanes, :]))
+
+    def send_first(j, inner):
+        send_row(first_out, first_in, 1 + CHUNKS, j, ahead(j))
+        return inner
+
+    lax.fori_loop(1, regions, send_first, 0)
+    edge_rows(0, edges)
+    for part, value in scatter(near_side, 0, keys):
+        grad_d[:, part] = value
+    grad_s[...] = dot_exact(scatter_hot[0:keys, near_side], rows_s[near_side, :])
+    back, edge_sem = send_edges_back(0)
+    sent += back
+    wait_rows(recv_sem, 0, regions - 1)
+    named = from_halves(small_in[...])
+    hot = one_hots(named[:, 24:25], slots)
+    gather_hot[pair_lanes : pair_lanes + slots, :] = hot.astype(BF16)
+    if slots < 128:
+        hot = jnp.concatenate([hot, jnp.zeros((128 - slots, hot.shape[1]), F32)], 0)
+        named = jnp.concatenate([named, jnp.ones((128 - slots, 128), F32)], 0)
+    scatter_hot[:, far_side] = jnp.transpose(hot[:, 0:128]).astype(BF16)
+    named = jnp.transpose(named)
+    pose[:, far_side] = named[0:8, :]
+    pmean[:, far_side] = named[8:16, :]
+    psq[:, far_side] = named[16:24, :]
+    pose_rows(pair_lanes, pair_coefs()[pair_lanes : pair_lanes + slots])
+    gather_cameras(pair_lanes, slots)
+    gather_depths(pair_lanes, slots)
+    take_edges(0, edge_sem)
+    gathers = []
+    shared = []
+    pending = None
+    tiles = TILES // CHUNKS
+    for h in range(CHUNKS):
+        wait_rows(recv_sem, 1 + h, chunk * (regions - 1))
+        begin, end = 128 * tiles * h, 128 * tiles * (h + 1)
+        for c in range(CAP):
+            for g in range(regions // 8):
+                at = pair_lanes + c * regions + 8 * g
+                for t in range(tiles * h, tiles * (h + 1)):
+                    for m in range(MAPS):
+                        source = MSG * 8 * g + CAP * MAPS * t + MAPS * c + m
+                        value = bulk_in[pl.ds(source, 8, stride=MSG), :]
+                        if m < 3:
+                            xs[m, at : at + 8, 128 * t : 128 * t + 128] = value
+                        else:
+                            cw[at : at + 8, 128 * t : 128 * t + 128] = value
+        groups(pair_lanes, slots, tiles * h, tiles * (h + 1))
+        for part, value in scatter(far_side, 0, own, begin, end):
+            grad_d[0:own, part] = grad_d[0:own, part] + value
+        shares = send_shares(0, begin, end)
+        shared += shares
+        if pending is not None:
+            gathers += update_depths(0, *pending)
+        pending = (begin, end, shares)
+    sums = grad_s[0:own, :] + dot_exact(scatter_hot[0:own, far_side], rows_s[far_side, :])
+    cameras = send_cameras(0, sums, back[1])
+    sent += cameras
+    send_sums(0)
+    gathers += update_depths(0, *pending)
+    update_cameras(0, cameras)
+    edges = [camera_coefs(1)]
+    gather_cameras(0, near_at)
+    gather_cameras(pair_lanes, slots)
+    update_pairs(0, True)
+    pair_rows(True)
+
+    for copy in gathers:
+        copy.wait_recv()
+    sent += gathers
+    edges.append(depths(1))
+    sent += edges
+    gather_depths(0, near_at)
+    gather_depths(pair_lanes, slots)
+    groups(0, near_at)
+    groups(pair_lanes, slots)
+    edge_rows(1, edges)
+    for copy in shared:
+        copy.wait_send()
+    rows = slice(0, total_rows)
+    for part, value in scatter(rows, 0, keys):
+        grad_d[:, part] = value
+    shares = send_shares(1, 0, ANCH)
+    grad_s[...] = dot_exact(scatter_hot[0:keys, rows], rows_s[rows, :])
+    back, edge_sem = send_edges_back(1)
+    send_sums(1)
+    cameras = send_cameras(1, grad_s[0:own, :], back[1])
+    take_edges(1, edge_sem)
+    gathers = update_depths(1, 0, ANCH, shares)
+    sent += shares + back + cameras
+    update_cameras(1, cameras)
+    update_pairs(1, False)
 
     wait_rows(send_sem, 0, regions - 1)
     for h in range(CHUNKS):
         wait_rows(send_sem, 1 + h, chunk * (regions - 1))
     for n in range(1 + ITERS):
         wait_rows(send_sem, 1 + CHUNKS + n, regions - 1)
+    for copy in sent:
+        copy.wait_send()
     cam_in[...] = cam[:, 0:own]
     pose_in[...] = pose[:, 0:pairs]
     pmean_in[...] = pmean[:, 0:pairs]
@@ -625,19 +720,26 @@
             )
         )
     ]
-    for store in stores:
+    for store in stores[1:]:
         store.start()
+    for copy in gathers:
+        copy.wait()
+    stores[0].start()
     for store in stores:
         store.wait()
 
 
 def deliver(*refs):
-    count = (len(refs) - 1) // 2
-    copies = [pltpu.make_async_copy(refs[n], refs[count + n], refs[-1].at[n]) for n in range(count)]
-    for copy in copies:
-        copy.start()
-    for copy in copies:
-        copy.wait()
+    sources, results, held, sems = refs[0:9], refs[9:18], refs[18:27], refs[27]
+    for bring in (True, False):
+        copies = [
+            pltpu.make_async_copy(sources[n] if bring else held[n], held[n] if bring else results[n], sems.at[n])
+            for n in range(9)
+        ]
+        for copy in copies:
+            copy.start()
+        for copy in copies:
+            copy.wait()
 
 
 def shards(
@@ -691,11 +793,11 @@
             vmem(regions, 128), vmem(regions, 128), vmem(MSG * regions, 128), vmem(MSG * regions, 128),
             vmem(regions, 128), vmem(regions, 128), vmem(ITERS, regions, 128), vmem(ITERS, regions, 128),
             vmem(ITERS, 2, EDGE, ANCH), vmem(ITERS, 2, EDGE, 128),
-            vmem(ITERS, 2, EDGE, ANCH), vmem(ITERS, 2, EDGE, 128),
-            vmem(ITERS, lanes - 1, share, ANCH), vmem(ITERS, lanes, 16, 128), vmem(2, 8, share),
+            vmem(ITERS, EDGE, ANCH), vmem(ITERS, 2, EDGE, 128),
+            vmem(ITERS, lanes - 1, share, ANCH), vmem(ITERS, lanes, EDGE, ANCH), vmem(ITERS, lanes, 16, 128), vmem(2, 8, share),
             pltpu.SemaphoreType.DMA((13,)),
             pltpu.SemaphoreType.DMA((2 + CHUNKS + ITERS,)), pltpu.SemaphoreType.DMA((2 + CHUNKS + ITERS,)),
-            pltpu.SemaphoreType.DMA((16 * ITERS,)), pltpu.SemaphoreType.DMA((16 * ITERS,)),
+            pltpu.SemaphoreType.DMA((48,)), pltpu.SemaphoreType.DMA((48,)),
         ],
         compiler_params=pltpu.CompilerParams(
             collective_id=0, has_side_effects=True, vmem_limit_bytes=62 * 1024 * 1024
@@ -711,7 +813,7 @@
         out_shape=shapes,
         in_specs=[in_hbm] * 9,
         out_specs=(in_hbm,) * 9,
-        scratch_shapes=[pltpu.SemaphoreType.DMA((9,))],
+        scratch_shapes=[vmem(*shape.shape) for shape in shapes] + [pltpu.SemaphoreType.DMA((9,))],
         compiler_params=pltpu.CompilerParams(vmem_limit_bytes=62 * 1024 * 1024),
         name="deliver",
     )(*results)

time: 99.6 us -> 96 us (0.964)
  Pallas kernels: 96.9 us -> 93 us
    pallas_call x1, Pallas kernels: 11.2 us -> 1.74 us  [shards(): pl.pallas_call(deliver, out_shape=shapes, in_specs=[in_hbm] * 9, out_spec...]
    pallas_call x1, Pallas kernels: 85.6 us -> 91.3 us  [shards(): pl.pallas_call(functools.partial(kernel, regions, lanes, own, pairs), out...]
where the time goes in v3:
time: 96 us; the launch traced here: 95.6 us
  Pallas kernels  93 us (97%)
  local copies, waits for them, and re-layouts  1.93 us (2%)
    pallas_call x1, Pallas kernels, shards(): pl.pallas_call(functools.partial(kernel, regions, lanes, own, pairs), out...  91.3 us
    unnamed x1, local copies, waits for them, and re-layouts  1.93 us

profile of v3, /device:TPU:4, one launch (start us, length us, event | category | flops | bytes accessed | tf_op | source)
XLA Modules:
  0.0 95.6 jit_solution(6813069424044746755)
XLA Ops:
  0.6 1.9 %copy.24 = bf16[190,2,768]{2,0,1:T(8,128)(2,1)} copy(bf16[190,2,768]{2,1,0:T(2,128)(2,1)} %param.23) | data formatting | bytes 1167360 | tf_op args[10]
  2.6 91.3 %align.1 = (f32[64,768]{1,0:T(8,128)}, f32[8,64]{1,0:T(8,128)}, f32[8,190]{1,0:T(8,128)}, f32[16,768]{1,0:T(8,128)}, f32[16,768]{1,0:T(8,128)}, /*index=5*/f32[8...) custom-call(f32[64,768]{1,0:T(8,128)} %logd_hbm.1, f32[8,64]{1,0:T(8,128)} %bitcast.23, ...), custom_call_target="tpu_custom_call" | custom-call | tf_op jit(solution)/shard_map/align/pallas_call | solution.py:772
  93.8 1.7 %deliver.1 = (f32[64,768]{1,0:T(8,128)}, f32[8,64]{1,0:T(8,128)}, f32[8,190]{1,0:T(8,128)}, f32[16,768]{1,0:T(8,128)}, f32[16,768]{1,0:T(8,128)}, /*index=5*/f32...) custom-call(f32[64,768]{1,0:T(8,128)} %get-tuple-element.27.refs_0_, ...), custom_call_target="tpu_custom_call" | custom-call | tf_op jit(solution)/shard_map/deliver/pallas_call | solution.py:811

commit v4 on v3

--- a/solution.py
+++ b/solution.py
@@ -235,7 +235,7 @@
     xs[...] = jnp.zeros_like(xs)
     cw[...] = jnp.zeros_like(cw)
     for m in range(MAPS):
-        source = points[3 + m] if m < 3 else conf[1]
+        source = points[3 + m] if m < 3 else conf[:, 1, :]
         chosen = dot(pick_hot[:, 0:pairs], source)
         if m == 3:
             chosen = chosen * slot_weights
@@ -264,75 +264,17 @@
         whole = bulk_in.at[pl.ds(0, count)]
         pltpu.make_async_copy(whole, whole, sem.at[which]).wait()
 
-    pl.semaphore_wait(barrier, regions - 1 + lanes - 1 + jnp.where(lane == 0, 0, 1))
-
-    def send_small(j, carry):
-        send_row(small_out, small_in, 0, j, ahead(j))
-        return carry
-
-    lax.fori_loop(1, regions, send_small, 0)
-    chunk = MSG // CHUNKS
-    for h in range(CHUNKS):
-
-        def send_chunk(j, carry, h=h):
-            at = pl.ds(pl.multiple_of((j - 1) * MSG + h * chunk, 8), chunk)
-            pltpu.make_async_remote_copy(
-                src_ref=bulk_out.at[at],
-                dst_ref=bulk_in.at[at],
-                send_sem=send_sem.at[1 + h],
-                recv_sem=recv_sem.at[1 + h],
-                device_id={"region": ahead(j)},
-            ).start()
-            return carry
-
-        def send_both(j, carry, send_chunk=send_chunk):
-            return send_chunk(regions - j, send_chunk(j, carry))
-
-        lax.fori_loop(1, regions // 2, send_both, 0)
-        send_chunk(regions // 2, 0)
-
-    for m in range(3):
-        xs[m, 0:pairs, :] = points[m].astype(F32)
-    cw[0:pairs, :] = conf[0].astype(F32) * weight_column[0:pairs]
     def one_hots(column, count):
         key_ids = lax.broadcasted_iota(jnp.int32, (count, gather_hot.shape[1]), 1)
         for n in (2, 1):
             key_ids = jnp.where(key_ids >= n * keys, jnp.where(key_ids < 3 * keys, key_ids - n * keys, -1), key_ids)
         return jnp.where(column == key_ids.astype(F32), 1.0, 0.0)
 
-    hot = one_hots(jnp.concatenate([as_column(firsts)[0:near_at], near], 0), pair_lanes)
-    gather_hot[0:pair_lanes, :] = hot.astype(BF16)
-    scatter_hot[:, 0:pair_lanes] = jnp.transpose(hot[:, 0:128]).astype(BF16)
-    place_ids = lax.broadcasted_iota(jnp.int32, back_hot.shape, 1).astype(F32)
-    back_hot[...] = jnp.where(as_column(place) == place_ids, 1.0, 0.0).astype(BF16)
-
     column_ids = lax.broadcasted_iota(jnp.int32, (8, 128), 1)
-    down_step = 8.0 * (128 // ANCH_W)
-    row_ids = lax.broadcasted_iota(jnp.int32, (128, 128), 0)
-    anchor = lax.broadcasted_iota(jnp.int32, (128, 128), 1)
-    anchor_row = lax.div(anchor, jnp.full_like(anchor, ANCH_W))
-    across = (8 * (anchor - anchor_row * ANCH_W) + 4 - 4 * ANCH_W).astype(F32)
-    downward = (8 * anchor_row + 4 - 4 * ANCH_H).astype(F32)
-    kind = lax.rem(row_ids, jnp.full_like(row_ids, COEFS))
-    kind = jnp.where(row_ids < 3 * COEFS, kind, -1)
-    for k in range(3):
-        ray = jnp.where(kind == 4 * k, across, jnp.where(kind == 4 * k + 1, downward, jnp.where(kind == 4 * k + 2, 1.0, 0.0)))
-        step = jnp.where(kind == 4 * k + 1, down_step, 0.0)
-        move = jnp.where(kind == 4 * k + 3, 1.0, 0.0)
-        for b, value in ((k, ray), (3 + k, step), (6 + k, move)):
-            camera_ones[:, 128 * b : 128 * b + 128] = value.astype(BF16)
-        for j in range(4):
-            b = 4 * k + j
-            pose_ones[:, 128 * b : 128 * b + 128] = jnp.where(kind == b, 1.0, 0.0).astype(BF16)
-    across = across[0:8, :]
-    downward = downward[0:8, :]
-
     for padded, values in ((cam, cam_in), (cmean, cmean_in), (csq, csq_in)):
         padded[...] = jnp.ones((8, 128), F32)
         padded[:, 0:own] = values[...]
     narrow[...] = jnp.zeros_like(narrow)
-    rows_g[...] = jnp.zeros_like(rows_g)
-    rows_s[...] = jnp.zeros_like(rows_s)
     table[...] = jnp.zeros_like(table)
     small_table[...] = jnp.zeros_like(small_table)
 
@@ -410,7 +352,7 @@
         return inner
 
     def groups(at, count, begin=0, end=TILES):
-        lax.fori_loop(at // 8, (at + count) // 8, functools.partial(group, begin=begin, end=end), 0)
+        lax.fori_loop(at // 8, (at + count) // 8, functools.partial(group, begin=begin, end=end), 0, unroll=4)
 
     def scatter(rows, keys_from, keys_to, begin=0, end=ANCH):
         hot = scatter_hot[keys_from:keys_to, rows]
@@ -432,10 +374,8 @@
             narrow[4 * k + 3 : 4 * k + 4, :] = cam[4 + k : 5 + k, :]
         coefs = jnp.transpose(narrow[...])[0:own, :]
         edge_c[it, 0] = coefs[0:EDGE, :]
-        copy = small_copy(edge_c.at[it, 0], edge_c.at[it, 1], {"region": behind(1)})
-        copy.start()
         fill(small_table, 0, coefs)
-        return copy
+        return small_copy(edge_c.at[it, 0], edge_c.at[it, 1], {"region": behind(1)})
 
     def pair_coefs():
         p = [pose[k : k + 1, :] for k in range(4)]
@@ -457,7 +397,8 @@
         depth = jnp.exp(logd[it])
         edge_d[it, 0] = depth[0:EDGE, :]
         copy = small_copy(edge_d.at[it, 0], edge_d.at[it, 1], {"region": behind(1)})
-        copy.start()
+        if it > 0:
+            copy.start()
         fill(table, 0, depth)
         return copy
 
@@ -596,8 +537,66 @@
     far_side = slice(pair_lanes, total_rows)
     sent = []
 
+
+    def send_chunk(h):
+        def send(j, carry):
+            at = pl.ds(pl.multiple_of((j - 1) * MSG + h * chunk, 8), chunk)
+            pltpu.make_async_remote_copy(
+                src_ref=bulk_out.at[at],
+                dst_ref=bulk_in.at[at],
+                send_sem=send_sem.at[1 + h],
+                recv_sem=recv_sem.at[1 + h],
+                device_id={"region": ahead(j)},
+            ).start()
+            return carry
+
+        lax.fori_loop(1, regions, send, 0)
+
     edges = [camera_coefs(0), depths(0)]
+    pl.semaphore_wait(barrier, regions - 1 + lanes - 1 + jnp.where(lane == 0, 0, 1))
+
+    def send_small(j, carry):
+        send_row(small_out, small_in, 0, j, ahead(j))
+        return carry
+
+    lax.fori_loop(1, regions, send_small, 0)
+    chunk = MSG // CHUNKS
+    for copy in edges:
+        copy.start()
     sent += edges
+    for h in range(CHUNKS - 1):
+        send_chunk(h)
+    for m in range(3):
+        xs[m, 0:pairs, :] = points[m].astype(F32)
+    cw[0:pairs, :] = conf[:, 0, :].astype(F32) * weight_column[0:pairs]
+    hot = one_hots(jnp.concatenate([as_column(firsts)[0:near_at], near], 0), pair_lanes)
+    gather_hot[0:pair_lanes, :] = hot.astype(BF16)
+    scatter_hot[:, 0:pair_lanes] = jnp.transpose(hot[:, 0:128]).astype(BF16)
+    place_ids = lax.broadcasted_iota(jnp.int32, back_hot.shape, 1).astype(F32)
+    back_hot[...] = jnp.where(as_column(place) == place_ids, 1.0, 0.0).astype(BF16)
+
+    down_step = 8.0 * (128 // ANCH_W)
+    row_ids = lax.broadcasted_iota(jnp.int32, (128, 128), 0)
+    anchor = lax.broadcasted_iota(jnp.int32, (128, 128), 1)
+    anchor_row = lax.div(anchor, jnp.full_like(anchor, ANCH_W))
+    across = (8 * (anchor - anchor_row * ANCH_W) + 4 - 4 * ANCH_W).astype(F32)
+    downward = (8 * anchor_row + 4 - 4 * ANCH_H).astype(F32)
+    kind = lax.rem(row_ids, jnp.full_like(row_ids, COEFS))
+    kind = jnp.where(row_ids < 3 * COEFS, kind, -1)
+    for k in range(3):
+        ray = jnp.where(kind == 4 * k, across, jnp.where(kind == 4 * k + 1, downward, jnp.where(kind == 4 * k + 2, 1.0, 0.0)))
+        step = jnp.where(kind == 4 * k + 1, down_step, 0.0)
+        move = jnp.where(kind == 4 * k + 3, 1.0, 0.0)
+        for b, value in ((k, ray), (3 + k, step), (6 + k, move)):
+            camera_ones[:, 128 * b : 128 * b + 128] = value.astype(BF16)
+        for j in range(4):
+            b = 4 * k + j
+            pose_ones[:, 128 * b : 128 * b + 128] = jnp.where(kind == b, 1.0, 0.0).astype(BF16)
+    across = across[0:8, :]
+    downward = downward[0:8, :]
+
+    rows_g[...] = jnp.zeros_like(rows_g)
+    rows_s[...] = jnp.zeros_like(rows_s)
     gather_depths(0, near_at)
     gather_cameras(0, near_at)
     pair_rows(False)
@@ -615,6 +614,7 @@
     grad_s[...] = dot_exact(scatter_hot[0:keys, near_side], rows_s[near_side, :])
     back, edge_sem = send_edges_back(0)
     sent += back
+    send_chunk(CHUNKS - 1)
     wait_rows(recv_sem, 0, regions - 1)
     named = from_halves(small_in[...])
     hot = one_hots(named[:, 24:25], slots)
@@ -630,10 +630,6 @@
     pose_rows(pair_lanes, pair_coefs()[pair_lanes : pair_lanes + slots])
     gather_cameras(pair_lanes, slots)
     gather_depths(pair_lanes, slots)
-    take_edges(0, edge_sem)
-    gathers = []
-    shared = []
-    pending = None
     tiles = TILES // CHUNKS
     for h in range(CHUNKS):
         wait_rows(recv_sem, 1 + h, chunk * (regions - 1))
@@ -652,18 +648,16 @@
         groups(pair_lanes, slots, tiles * h, tiles * (h + 1))
         for part, value in scatter(far_side, 0, own, begin, end):
             grad_d[0:own, part] = grad_d[0:own, part] + value
-        shares = send_shares(0, begin, end)
-        shared += shares
-        if pending is not None:
-            gathers += update_depths(0, *pending)
-        pending = (begin, end, shares)
+    shares = send_shares(0, 0, ANCH)
     sums = grad_s[0:own, :] + dot_exact(scatter_hot[0:own, far_side], rows_s[far_side, :])
     cameras = send_cameras(0, sums, back[1])
     sent += cameras
     send_sums(0)
-    gathers += update_depths(0, *pending)
+    take_edges(0, edge_sem)
+    gathers = update_depths(0, 0, ANCH, shares)
     update_cameras(0, cameras)
     edges = [camera_coefs(1)]
+    edges[0].start()
     gather_cameras(0, near_at)
     gather_cameras(pair_lanes, slots)
     update_pairs(0, True)
@@ -679,7 +673,7 @@
     groups(0, near_at)
     groups(pair_lanes, slots)
     edge_rows(1, edges)
-    for copy in shared:
+    for copy in shares:
         copy.wait_send()
     rows = slice(0, total_rows)
     for part, value in scatter(rows, 0, keys):
@@ -780,7 +774,7 @@
             vmem(ITERS + 1, own, ANCH), vmem(share, ANCH), vmem(share, ANCH),
             vmem(8, 128), vmem(8, 128), vmem(8, 128),
             vmem(8, total_rows), vmem(8, total_rows), vmem(8, total_rows),
-            vmem(6, pairs, ANCH, dtype=BF16), vmem(2, pairs, ANCH, dtype=BF16),
+            vmem(6, pairs, ANCH, dtype=BF16), vmem(pairs, 2, ANCH, dtype=BF16),
             vmem(3, total_rows, ANCH), vmem(total_rows, ANCH),
             vmem(8, pair_lanes, dtype=jnp.int32),
             vmem(slots + nearby, pair_lanes, dtype=BF16), vmem(pair_lanes, slots + nearby, dtype=BF16),
@@ -805,7 +799,7 @@
         name="align",
     )(
         log_depth, cameras.T, pair_pose.T, depth_mean, depth_square, camera_mean.T, camera_square.T,
-        pose_mean.T, pose_square.T, pointmaps.transpose(1, 0, 2), confidence.transpose(1, 0, 2),
+        pose_mean.T, pose_square.T, pointmaps.transpose(1, 0, 2), confidence,
         pair_images.T, pair_flag.reshape(1, pairs),
     )
     depth, camera, pose, dmean, dsq, cmean, csq, pmean, psq = pl.pallas_call(

time: 96 us -> 79.7 us (0.83)
  Pallas kernels: 93 us -> 78.9 us
  local copies, waits for them, and re-layouts: 1.93 us -> 0 us
    pallas_call x1, Pallas kernels: 91.3 us -> 77.1 us  [shards(): pl.pallas_call(functools.partial(kernel, regions, lanes, own, pairs), out...]
    unnamed x1 -> x0, local copies, waits for them, and re-layouts: 1.93 us -> none
where the time goes in v4:
time: 79.7 us; the launch traced here: 79.5 us
  Pallas kernels  78.9 us (99%)
    pallas_call x1, Pallas kernels, shards(): pl.pallas_call(functools.partial(kernel, regions, lanes, own, pairs), out...  77.1 us
    pallas_call x1, Pallas kernels, shards(): pl.pallas_call(deliver, out_shape=shapes, in_specs=[in_hbm] * 9, out_spec...  1.74 us

profile of v4, /device:TPU:4, one launch (start us, length us, event | category | flops | bytes accessed | tf_op | source)
XLA Modules:
  0.0 79.5 jit_solution(2337526260050257942)
XLA Ops:
  0.6 77.1 %align.1 = (f32[64,768]{1,0:T(8,128)}, f32[8,64]{1,0:T(8,128)}, f32[8,190]{1,0:T(8,128)}, f32[16,768]{1,0:T(8,128)}, f32[16,768]{1,0:T(8,128)}, /*index=5*/f32[8...) custom-call(f32[64,768]{1,0:T(8,128)} %logd_hbm.1, f32[8,64]{1,0:T(8,128)} %bitcast.19, ...), custom_call_target="tpu_custom_call" | custom-call | tf_op jit(solution)/shard_map/align/pallas_call | solution.py:766
  77.8 1.7 %deliver.1 = (f32[64,768]{1,0:T(8,128)}, f32[8,64]{1,0:T(8,128)}, f32[8,190]{1,0:T(8,128)}, f32[16,768]{1,0:T(8,128)}, f32[16,768]{1,0:T(8,128)}, /*index=5*/f32...) custom-call(f32[64,768]{1,0:T(8,128)} %get-tuple-element.27.refs_0_, ...), custom_call_target="tpu_custom_call" | custom-call | tf_op jit(solution)/shard_map/deliver/pallas_call | solution.py:805

commit v5 on v4

--- a/solution.py
+++ b/solution.py
@@ -632,6 +632,8 @@
     gather_depths(pair_lanes, slots)
     tiles = TILES // CHUNKS
     for h in range(CHUNKS):
+        if h == CHUNKS - 1:
+            early = send_shares(0, 0, 128 * tiles * h)
         wait_rows(recv_sem, 1 + h, chunk * (regions - 1))
         begin, end = 128 * tiles * h, 128 * tiles * (h + 1)
         for c in range(CAP):
@@ -648,13 +650,14 @@
         groups(pair_lanes, slots, tiles * h, tiles * (h + 1))
         for part, value in scatter(far_side, 0, own, begin, end):
             grad_d[0:own, part] = grad_d[0:own, part] + value
-    shares = send_shares(0, 0, ANCH)
+    shares = send_shares(0, begin, ANCH)
     sums = grad_s[0:own, :] + dot_exact(scatter_hot[0:own, far_side], rows_s[far_side, :])
     cameras = send_cameras(0, sums, back[1])
     sent += cameras
     send_sums(0)
     take_edges(0, edge_sem)
-    gathers = update_depths(0, 0, ANCH, shares)
+    gathers = update_depths(0, 0, begin, early)
+    gathers += update_depths(0, begin, ANCH, shares)
     update_cameras(0, cameras)
     edges = [camera_coefs(1)]
     edges[0].start()
@@ -673,19 +676,23 @@
     groups(0, near_at)
     groups(pair_lanes, slots)
     edge_rows(1, edges)
-    for copy in shares:
+    for copy in early + shares:
         copy.wait_send()
     rows = slice(0, total_rows)
+    shares = []
     for part, value in scatter(rows, 0, keys):
         grad_d[:, part] = value
-    shares = send_shares(1, 0, ANCH)
+        shares.append((part.start, part.stop, send_shares(1, part.start, part.stop)))
     grad_s[...] = dot_exact(scatter_hot[0:keys, rows], rows_s[rows, :])
     back, edge_sem = send_edges_back(1)
     send_sums(1)
     cameras = send_cameras(1, grad_s[0:own, :], back[1])
     take_edges(1, edge_sem)
-    gathers = update_depths(1, 0, ANCH, shares)
-    sent += shares + back + cameras
+    gathers = []
+    for share_part in shares:
+        gathers += update_depths(1, *share_part)
+        sent += share_part[2]
+    sent += back + cameras
     update_cameras(1, cameras)
     update_pairs(1, False)
 
@@ -791,7 +798,7 @@
             vmem(ITERS, lanes - 1, share, ANCH), vmem(ITERS, lanes, EDGE, ANCH), vmem(ITERS, lanes, 16, 128), vmem(2, 8, share),
             pltpu.SemaphoreType.DMA((13,)),
             pltpu.SemaphoreType.DMA((2 + CHUNKS + ITERS,)), pltpu.SemaphoreType.DMA((2 + CHUNKS + ITERS,)),
-            pltpu.SemaphoreType.DMA((48,)), pltpu.SemaphoreType.DMA((48,)),
+            pltpu.SemaphoreType.DMA((64,)), pltpu.SemaphoreType.DMA((64,)),
         ],
         compiler_params=pltpu.CompilerParams(
             collective_id=0, has_side_effects=True, vmem_limit_bytes=62 * 1024 * 1024

time: 79.7 us -> 80.1 us (level)
  no operation moved by 1% of the time
where the time goes in v5:
time: 80.1 us; the launch traced here: 80 us
  Pallas kernels  79.4 us (99%)
    pallas_call x1, Pallas kernels, shards(): pl.pallas_call(functools.partial(kernel, regions, lanes, own, pairs), out...  77.6 us
    pallas_call x1, Pallas kernels, shards(): pl.pallas_call(deliver, out_shape=shapes, in_specs=[in_hbm] * 9, out_spec...  1.74 us

profile of v5, /device:TPU:4, one launch (start us, length us, event | category | flops | bytes accessed | tf_op | source)
XLA Modules:
  0.0 80.0 jit_solution(5855977510669677291)
XLA Ops:
  0.6 77.6 %align.1 = (f32[64,768]{1,0:T(8,128)}, f32[8,64]{1,0:T(8,128)}, f32[8,190]{1,0:T(8,128)}, f32[16,768]{1,0:T(8,128)}, f32[16,768]{1,0:T(8,128)}, /*index=5*/f32[8...) custom-call(f32[64,768]{1,0:T(8,128)} %logd_hbm.1, f32[8,64]{1,0:T(8,128)} %bitcast.19, ...), custom_call_target="tpu_custom_call" | custom-call | tf_op jit(solution)/shard_map/align/pallas_call | solution.py:773
  78.3 1.7 %deliver.1 = (f32[64,768]{1,0:T(8,128)}, f32[8,64]{1,0:T(8,128)}, f32[8,190]{1,0:T(8,128)}, f32[16,768]{1,0:T(8,128)}, f32[16,768]{1,0:T(8,128)}, /*index=5*/f32...) custom-call(f32[64,768]{1,0:T(8,128)} %get-tuple-element.27.refs_0_, ...), custom_call_target="tpu_custom_call" | custom-call | tf_op jit(solution)/shard_map/deliver/pallas_call | solution.py:812
